TPU v7x, 256 devices: a whole 4x4x8 slice. The times are simulated.
256 devices in a mesh: comp: 64 (over z, y, x_lo), band: 4 (over x_hi, core).
Axes of the slice: x: 4 (x_hi: 2, x_lo: 2; x = x_hi * 2 + x_lo), y: 4, z: 8, core: 2. Of those that a mesh axis runs over, the one named last changes fastest.
Arguments:
- spectrum: float32 [1152, 32, 4096], P('comp', 'band'), may hold values from 0.1 to 1
- currents: float32 [2, 32, 4096], P(None, 'band', 'comp'), may hold values from -4 to 4
- group_courant: float32 [32], replicated, may hold values from 0.1 to 0.35
- refraction: float32 [8, 32], replicated, may hold values from -0.25 to 0.25
- interp: float32 [1152, 1152], replicated, may hold values from -0.1875 to 0.1875
- sea_mask: int32 [32, 4096], replicated, may hold values 0 or 1
- depth_class: int32 [32, 4096], replicated, may hold values from 0 to 7
- owner_map: int32 [64], replicated, may hold values from 0 to 63, each once
Outputs:
- spectrum_out: float32 [1152, 32, 4096], P('comp', 'band')
- ocean_out: float32 [2, 32, 4096], P(None, 'band', 'comp')
Inputs may be any that keep to these rules, and one draw needn't show every extreme that they name: `owner_map`: each of 0 to 63 once.
All inputs are finite; a program needn't handle non-finite values.
Results may differ from a plain program's by a relative error of at most 0.000098.
Values sent between devices are 32-bit elements; how exact they have to be, the bound alone decides.
A program may use at most 128 MiB of HBM per device.

v0:
```python
import math

import jax
import jax.numpy as jnp
from jax import lax
from jax.sharding import PartitionSpec as P

DIRS = 36
FREQ = 32
SUBSTEPS = 4


CURRENT_COURANT = 0.025
SOURCE_STEP = 0.5
STOKES_SCALE = 0.2
OCEAN_STEP = 0.5
VISCOSITY = 0.2
DRAG = 0.1
HIGHEST = lax.Precision.HIGHEST


def swapped(block, axis, apart):
    count = lax.axis_size(axis)
    route = []
    for low in range(count):
        high = low | 1 << apart
        if high != low and high < count:
            route += [(low, high), (high, low)]
    return lax.ppermute(block, axis, route)


def padded_2(value, sides, width):
    for axis, dim in sides:
        count, length = (lax.axis_size(axis), value.shape[dim])
        up = [(i, (i + 1) % count) for i in range(count - 1)]
        down = [(j, i) for i, j in up]
        last = lax.slice_in_dim(value, length - width, length, axis=dim)
        first = lax.slice_in_dim(value, 0, width, axis=dim)
        before = lax.ppermute(last, axis, up)
        after = lax.ppermute(first, axis, down)
        value = jnp.concatenate([before, value, after], axis=dim)
    return value


def from_everyone(value, axis):
    count = lax.axis_size(axis)
    return lax.all_to_all(
        jnp.broadcast_to(value[None], (count, *value.shape)), axis, 0, 0, tiled=True
    )


def laid_out(pieces, dim):
    dims = list(pieces.shape[1:])
    dims[dim] *= pieces.shape[0]
    return jnp.moveaxis(pieces, 0, dim).reshape(dims)


def gather_directly(value, axis, dim):
    pieces = from_everyone(value, axis)
    return laid_out(pieces, dim)


def reorder_tiles(values_in, tile_order, tile_count):
    lead_dim, row_count, col_count = values_in.shape
    pieces = values_in.reshape(lead_dim, row_count, tile_count, col_count // tile_count)
    return jnp.take(pieces, tile_order, axis=2).reshape(lead_dim, row_count, col_count)


def upwind(centre_val, behind, ahead_val, speeds):
    return jnp.maximum(speeds, 0.0) * (centre_val - behind) + jnp.minimum(speeds, 0.0) * (
        ahead_val - centre_val
    )


def direction_pair(centre):
    dir_count, row_count, col_count = centre.shape
    edge_dirs = jnp.stack([centre[0], centre[dir_count - 1]])
    partner = swapped(edge_dirs, "comp", 0)
    before_dir = jnp.concatenate([partner[1:2], centre[: dir_count - 1]], axis=0)
    after_dir = jnp.concatenate([centre[1:], partner[0:1]], axis=0)
    return (before_dir, after_dir)


def advance(padded, lon_speed, lat_speed, dir_speed, ocean_rows):
    centre = padded[:, 1:-1]
    south_rows = padded[:, :-2]
    north_rows = padded[:, 2:]
    west_cols = jnp.roll(centre, 1, axis=2)
    east_cols = jnp.roll(centre, -1, axis=2)
    before_dir, after_dir = direction_pair(centre)
    change = (
        upwind(centre, west_cols, east_cols, lon_speed)
        + upwind(centre, south_rows, north_rows, lat_speed)
        + upwind(centre, before_dir, after_dir, dir_speed)
    )
    return ocean_rows[None] * (centre - change)


def coefficients(current_rows, class_rows, speeds, cosine, sines, columns):
    lon_speed = (
        speeds[:, None, None] * cosine[:, None, None] + CURRENT_COURANT * current_rows[0][None]
    )
    lat_speed = (
        speeds[:, None, None] * sines[:, None, None] + CURRENT_COURANT * current_rows[1][None]
    )
    turning = jnp.zeros((speeds.shape[0],) + class_rows.shape, jnp.float32)
    for level in range(columns.shape[0]):
        turning = (
            turning
            + (class_rows == level).astype(jnp.float32)[None] * columns[level][:, None, None]
        )
    return (lon_speed, lat_speed, turning * cosine[:, None, None])


def component_tables(component, group_courant, refraction):
    frequency = component // DIRS
    direction = component % DIRS
    angles = direction.astype(jnp.float32) * (2.0 * math.pi / DIRS)
    return (
        jnp.take(group_courant, frequency),
        jnp.cos(angles),
        jnp.sin(angles),
        jnp.take(refraction, frequency, axis=1),
    )


def stokes_weights(comp_total):
    component = jnp.arange(comp_total, dtype=jnp.int32)
    frequency = component // DIRS
    direction = component % DIRS
    angles = direction.astype(jnp.float32) * (2.0 * math.pi / DIRS)
    scales = STOKES_SCALE * (frequency + 1).astype(jnp.float32) / FREQ
    return jnp.stack([scales * jnp.cos(angles), scales * jnp.sin(angles)])


def source_local(points, interp, weights):
    comp_total, row_count, col_count = points.shape
    flat_spec = points.reshape(comp_total, row_count * col_count)
    forward = jnp.dot(interp, flat_spec, precision=HIGHEST, preferred_element_type=jnp.float32)
    backward = lax.dot_general(
        interp,
        flat_spec,
        (((0,), (0,)), ((), ())),
        precision=HIGHEST,
        preferred_element_type=jnp.float32,
    )
    updated = flat_spec + SOURCE_STEP * (
        forward * backward - 0.5 * flat_spec * (forward + backward)
    )
    drift_rows = jnp.dot(weights, updated, precision=HIGHEST, preferred_element_type=jnp.float32)
    return (
        updated.reshape(comp_total, row_count, col_count),
        drift_rows.reshape(2, row_count, col_count),
    )


def velocity_rows(current_real):
    return padded_2(current_real, (("band", 1),), 1)


def ocean_update(current_rows, ocean_rows, tile_index, tile_width, stokes, coriolis):
    wrapped = jnp.concatenate(
        [current_rows[:, :, -1:], current_rows, current_rows[:, :, :1]], axis=2
    )
    ocean_wrapped = jnp.concatenate([ocean_rows[:, -1:], ocean_rows, ocean_rows[:, :1]], axis=1)
    tile_start = tile_index * tile_width
    cur_tile = lax.dynamic_slice_in_dim(wrapped, tile_start, tile_width + 2, 2)
    ocean_tile = lax.dynamic_slice_in_dim(ocean_wrapped, tile_start, tile_width + 2, 1)
    masked_cur = cur_tile * ocean_tile[None]
    centre = masked_cur[:, 1:-1, 1:-1]
    laplace = (
        masked_cur[:, 1:-1, :-2]
        + masked_cur[:, 1:-1, 2:]
        + masked_cur[:, :-2, 1:-1]
        + masked_cur[:, 2:, 1:-1]
        - 4.0 * centre
    )
    sea_tile = ocean_tile[1:-1, 1:-1]
    east_new = sea_tile * (
        centre[0]
        + OCEAN_STEP
        * (coriolis * (centre[1] + stokes[1]) + VISCOSITY * laplace[0] - DRAG * centre[0])
    )
    north_new = sea_tile * (
        centre[1]
        + OCEAN_STEP
        * (-coriolis * (centre[0] + stokes[0]) + VISCOSITY * laplace[1] - DRAG * centre[1])
    )
    return jnp.stack([east_new, north_new])


def local(spectrum, currents, group_courant, refraction, interp, sea_mask, depth_class, owner_map):
    per_device, rows_dev, lon_cells = spectrum.shape
    tile_count = lax.axis_size("comp")
    tile_width = lon_cells // tile_count
    band_pos = lax.axis_index("band")
    comp_pos = lax.axis_index("comp")
    inverse = jnp.argsort(owner_map)
    gathered = gather_directly(currents, "comp", 2)
    current_real = reorder_tiles(gathered, inverse, tile_count)
    ocean_pad = jnp.pad(sea_mask.astype(jnp.float32), ((SUBSTEPS, SUBSTEPS), (0, 0)))
    class_pad = jnp.pad(depth_class, ((SUBSTEPS, SUBSTEPS), (0, 0)))
    own_start = band_pos * rows_dev + SUBSTEPS
    ocean_own = lax.dynamic_slice_in_dim(ocean_pad, own_start, rows_dev, 0)
    class_own = lax.dynamic_slice_in_dim(class_pad, own_start, rows_dev, 0)
    weights = stokes_weights(interp.shape[0])
    component = comp_pos * per_device + jnp.arange(per_device, dtype=jnp.int32)
    speeds, cosine, sines, columns = component_tables(component, group_courant, refraction)
    wave_state = spectrum * ocean_own[None]
    lon_speed, lat_speed, dir_speed = coefficients(
        current_real, class_own, speeds, cosine, sines, columns
    )
    for substep in range(SUBSTEPS):
        padded = padded_2(wave_state, (("band", 1),), 1)
        wave_state = advance(padded, lon_speed, lat_speed, dir_speed, ocean_own)
    current_rows = velocity_rows(current_real)
    block_len = rows_dev * lon_cells // tile_count
    blocked = wave_state.reshape(per_device, tile_count, block_len)
    points = lax.all_to_all(blocked, "comp", split_axis=1, concat_axis=0, tiled=True)
    updated, drift_block = source_local(points, interp, weights)
    returned = lax.all_to_all(updated, "comp", split_axis=0, concat_axis=1, tiled=True)
    spectrum_out = returned.reshape(per_device, rows_dev, lon_cells)
    drift_all = gather_directly(drift_block, "comp", 1).reshape(2, rows_dev, lon_cells)
    stokes = lax.dynamic_slice_in_dim(drift_all, owner_map[comp_pos] * tile_width, tile_width, 2)
    ocean_rows = lax.dynamic_slice_in_dim(ocean_pad, own_start - 1, rows_dev + 2, 0)
    total_rows = sea_mask.shape[0]
    row_global = band_pos * rows_dev + jnp.arange(rows_dev, dtype=jnp.int32)
    latitude = -1.2 + 2.4 * (row_global.astype(jnp.float32) + 0.5) / total_rows
    coriolis = jnp.sin(latitude)[:, None]
    tile_index = owner_map[comp_pos]
    ocean_out = ocean_update(current_rows, ocean_rows, tile_index, tile_width, stokes, coriolis)
    return (spectrum_out, ocean_out)


def solution(mesh):
    in_specs = (P("comp", "band", None), P(None, "band", "comp"), P(), P(), P(), P(), P(), P())
    out_specs = (P("comp", "band", None), P(None, "band", "comp"))
    return jax.shard_map(local, mesh=mesh, in_specs=in_specs, out_specs=out_specs, check_vma=False)
```

profile of v0, /device:TPU:1, one launch (start us, length us, event | category | flops | bytes accessed | tf_op | source)
XLA Modules:
  0.0 376.3 jit_solution(10272515324481727480)
XLA Ops:
  1.4 1.0 reshape.282
  2.4 13.8 %all-to-all-start = ((f32[64,1,1024]{2,1,0:T(1,128)}), f32[64,1,1024]{2,1,0:T(1,128)}, u32[]{:S(2)}, u32[]{:S(2)}) async-start(f32[64,1,1024]{2,1,0:T(1,128)} %reshape.282), calls=%async_computation | async-start | bytes 524288 | tf_op jit(solution)/shard_map/all_to_all | solution.py:47
  16.3 1.1 convert_element_type.84
  18.2 3.1 copy_multiply_fusion
  22.4 0.9 collective-permute-start.2
  23.3 1.0 fusion.120
  24.3 5.7 %collective-permute-start = (f32[18,1,4096]{2,0,1:T(8,128)}, f32[18,1,4096]{2,0,1:T(8,128)}, u32[]{:S(2)}, u32[]{:S(2)}) collective-permute-start(f32[18,1,4096]{2,0,1:T(8,128)} %get-tuple-element.50), channel_id=1, source_target_pairs={{0,1},{1,2},{2,3},{4,5},{5,6},{6,7},{8,9},{9,10},{10,11},{12,13},{... | collective-permute-start | bytes 884744 | tf_op jit(solution)/shard_map/ppermute | solution.py:39
  30.0 2.1 collective-permute-start.1
  32.2 2.0 sort.17
  35.4 3.8 %fusion.118 = (f32[18,8,4095]{2,0,1:T(8,128)}, f32[18,8,4095]{2,0,1:T(8,128)}) fusion(f32[18,8,4096]{2,0,1:T(8,128)S(1)} %copy_multiply_fusion), kind=kLoop, calls=%fused_computation.217 | loop fusion | bytes 9434880 | tf_op jit(solution)/shard_map/jit(_roll_static)/slice | solution.py:89
  39.2 3.2 fusion.116
  44.5 0.9 slice_reduce_fusion.7
  45.4 3.5 compare_convert_fusion.7
  48.9 1.2 pad_clamp_fusion
  50.8 1.0 fusion.126
  53.9 2.9 reduce.16
  56.8 1.9 reshape.283
  58.7 1.9 copy.82
  60.6 2.6 gather_fusion.1
  63.2 1.2 broadcast_select_fusion
  65.9 1.7 mul.423
  67.6 1.7 copy.54
  69.3 1.7 mul.428
  71.0 11.5 %fusion.20 = f32[18,8,4096]{2,0,1:T(8,128)S(1)} fusion(f32[18,8,4096]{2,0,1:T(8,128)S(1)} %copy_multiply_fusion, f32[18,1,4096]{2,0,1:T(8,128)} %collective-permute-done.1, f32[18,1,4096]{2,0,1:T(8,128)} %collective-permute-done, f32[18,8,4095]{2,0,1:T(8,128)} %get-tuple-element.47, f32[18,8,1]{2,0,1:T(8,128)} %get-tuple-element.49, ...), kind=kLoop, calls=%fused_computation.27 | loop fusion | flops 28901376 | bytes 16188184 | tf_op jit(solution)/shard_map/mul | solution.py:96
  82.7 1.1 fusion.113
  85.1 5.2 %collective-permute-start.3 = (f32[18,1,4096]{2,0,1:T(8,128)S(1)}, f32[18,1,4096]{2,0,1:T(8,128)S(1)}, u32[]{:S(2)}, u32[]{:S(2)}) collective-permute-start(f32[18,1,4096]{2,0,1:T(8,128)S(1)} %get-tuple-element.40), channel_id=1, source_target_pairs={{0,1},{1,2},{2,3},{4,5},{5,6},{6,7},{8,9},{9,10},{10,11},{12,13},{... | collective-permute-start | bytes 884744 | tf_op jit(solution)/shard_map/ppermute | solution.py:39
  90.3 2.1 collective-permute-start.4
  92.9 2.1 collective-permute-done.3
  95.0 5.9 %collective-permute-done.4 = f32[18,1,4096]{2,0,1:T(8,128)S(1)} collective-permute-done((f32[18,1,4096]{2,0,1:T(8,128)S(1)}, f32[18,1,4096]{2,0,1:T(8,128)S(1)}, u32[]{:S(2)}, u32[]{:S(2)}) %collective-permute-start.4) | collective-permute-done | bytes 294944 | tf_op jit(solution)/shard_map/ppermute | solution.py:40
  101.1 8.2 %fusion.25 = f32[18,8,4096]{2,0,1:T(8,128)S(1)} fusion(f32[18,8,4096]{2,0,1:T(8,128)S(1)} %fusion.20, f32[18,1,4096]{2,0,1:T(8,128)S(1)} %collective-permute-done.4, f32[18,1,4096]{2,0,1:T(8,128)S(1)} %collective-permute-done.3, f32[18,8,4095]{2,0,1:T(8,128)S(1)} %get-tuple-element.37, f32[18,8,1]{2,0,1:T(8,128)S(1)} %get-tuple-element.39, ...), kind=kLoop, calls=%fused_computation.32 | loop fusion | flops 28901376 | bytes 16188184 | tf_op jit(solution)/shard_map/mul | solution.py:96
  109.4 1.1 fusion.108
  112.3 2.6 collective-permute-start.6
  114.9 1.9 collective-permute-start.7
  117.3 2.5 collective-permute-done.6
  119.8 5.8 %collective-permute-done.7 = f32[18,1,4096]{2,0,1:T(8,128)S(1)} collective-permute-done((f32[18,1,4096]{2,0,1:T(8,128)S(1)}, f32[18,1,4096]{2,0,1:T(8,128)S(1)}, u32[]{:S(2)}, u32[]{:S(2)}) %collective-permute-start.7) | collective-permute-done | bytes 294944 | tf_op jit(solution)/shard_map/ppermute | solution.py:40
  125.5 8.1 %fusion.30 = f32[18,8,4096]{2,0,1:T(8,128)S(1)} fusion(f32[18,8,4096]{2,0,1:T(8,128)S(1)} %fusion.25, f32[18,1,4096]{2,0,1:T(8,128)S(1)} %collective-permute-done.7, f32[18,1,4096]{2,0,1:T(8,128)S(1)} %collective-permute-done.6, f32[18,8,4095]{2,0,1:T(8,128)S(1)} %get-tuple-element.27, f32[18,8,1]{2,0,1:T(8,128)S(1)} %get-tuple-element.29, ...), kind=kLoop, calls=%fused_computation.37 | loop fusion | flops 28901376 | bytes 16188184 | tf_op jit(solution)/shard_map/mul | solution.py:96
  133.8 1.1 fusion.103
  136.2 2.6 collective-permute-start.9
  138.9 1.9 collective-permute-start.10
  141.6 2.1 collective-permute-done.9
  143.7 5.8 %collective-permute-done.10 = f32[18,1,4096]{2,0,1:T(8,128)S(1)} collective-permute-done((f32[18,1,4096]{2,0,1:T(8,128)S(1)}, f32[18,1,4096]{2,0,1:T(8,128)S(1)}, u32[]{:S(2)}, u32[]{:S(2)}) %collective-permute-start.10) | collective-permute-done | bytes 294944 | tf_op jit(solution)/shard_map/ppermute | solution.py:40
  149.5 8.0 %fusion.35 = f32[18,8,4096]{2,0,1:T(8,128)S(1)} fusion(f32[18,8,4096]{2,0,1:T(8,128)S(1)} %fusion.30, f32[18,1,4096]{2,0,1:T(8,128)S(1)} %collective-permute-done.10, f32[18,1,4096]{2,0,1:T(8,128)S(1)} %collective-permute-done.9, f32[18,8,4095]{2,0,1:T(8,128)S(1)} %get-tuple-element.17, f32[18,8,1]{2,0,1:T(8,128)S(1)} %get-tuple-element.19, ...), kind=kLoop, calls=%fused_computation.42 | loop fusion | flops 28901376 | bytes 16188184 | tf_op jit(solution)/shard_map/mul | solution.py:96
  157.5 1.4 copy.72
  158.9 1.6 reshape.245
  160.6 4.7 %copy.73 = f32[18,64,512]{2,0,1:T(8,128)} copy(f32[18,64,512]{2,1,0:T(8,128)} %reshape.245) | data formatting | bytes 4718592 | tf_op jit(solution)/shard_map/reshape | solution.py:218
  165.3 10.2 %all-to-all-start.1 = ((f32[18,64,512]{2,0,1:T(8,128)}), f32[18,64,512]{2,0,1:T(8,128)S(1)}, u32[]{:S(2)}, u32[]{:S(2)}) async-start(f32[18,64,512]{2,0,1:T(8,128)} %copy.73), calls=%async_computation.1 | async-start | bytes 6291456 | tf_op jit(solution)/shard_map/all_to_all | solution.py:219
  175.7 67.8 %all-to-all-done.1 = f32[18,64,512]{2,0,1:T(8,128)S(1)} async-done(((f32[18,64,512]{2,0,1:T(8,128)}), f32[18,64,512]{2,0,1:T(8,128)S(1)}, u32[]{:S(2)}, u32[]{:S(2)}) %all-to-all-start.1) | async-done | bytes 2359328 | tf_op jit(solution)/shard_map/all_to_all | solution.py:219
  243.5 1.6 reshape.246
  245.0 2.5 copy.75
  247.6 14.6 %fusion.128 = f32[512,1152]{1,0:T(8,128)S(1)} fusion(f32[1152,512]{1,0:T(8,128)} %reshape.246, f32[1152,1152]{1,0:T(8,128)} %param.12), kind=kOutput, calls=%fused_computation.227 | convolution fusion | flops 8153726976 | bytes 10027008 | tf_op jit(solution)/shard_map/dot_general | solution.py:140
  262.2 22.8 %fusion.127 = f32[512,1152]{1,0:T(8,128)S(1)} fusion(f32[1152,512]{1,0:T(8,128)S(1)} %copy-done.2, f32[1152,1152]{1,0:T(8,128)} %param.12), kind=kOutput, calls=%fused_computation.226 | convolution fusion | flops 8153726976 | bytes 10027008 | tf_op jit(solution)/shard_map/dot_general | solution.py:139
  285.1 2.4 fusion.63
  288.2 6.2 %all-to-all-start.3 = ((f32[64,2,1,512]{3,1,2,0:T(2,128)}), f32[64,2,1,512]{3,1,2,0:T(2,128)}, u32[]{:S(2)}, u32[]{:S(2)}) async-start(f32[64,2,1,512]{3,1,2,0:T(2,128)} %broadcast_in_dim.73), calls=%async_computation.3 | async-start | bytes 524288 | tf_op jit(solution)/shard_map/all_to_all | solution.py:47
  294.5 4.5 %fusion.100 = f32[1152,1,512]{0,2,1:T(8,128)} fusion(f32[1152,512]{0,1:T(8,128)S(1)} %copy.75, f32[512,1152]{1,0:T(8,128)} %copy-done.4, f32[512,1152]{1,0:T(8,128)} %copy-done.3), kind=kLoop, calls=%fused_computation.199 | loop fusion | flops 4128768 | bytes 9437184 | tf_op jit(solution)/shard_map/reshape | solution.py:152
  299.0 6.4 %copy.76 = f32[1152,1,512]{2,1,0:T(1,128)} copy(f32[1152,1,512]{0,2,1:T(8,128)} %fusion.100) | data formatting | bytes 4718592 | tf_op jit(solution)/shard_map/reshape | solution.py:152
  305.5 10.7 %all-to-all-start.2 = ((f32[1152,1,512]{2,1,0:T(1,128)}), f32[1152,1,512]{2,1,0:T(1,128)S(1)}, u32[]{:S(2)}, u32[]{:S(2)}) async-start(f32[1152,1,512]{2,1,0:T(1,128)} %copy.76), calls=%async_computation.2 | async-start | bytes 4718592 | tf_op jit(solution)/shard_map/all_to_all | solution.py:221
  318.4 1.1 concatenate.111
  320.7 2.0 collective-permute-start.12
  322.7 2.3 collective-permute-start.13
  325.1 4.6 %collective-permute-done.13 = f32[2,1,4096]{2,1,0:T(1,128)S(1)} collective-permute-done((f32[2,1,4096]{2,1,0:T(1,128)S(1)}, f32[2,1,4096]{2,1,0:T(1,128)S(1)}, u32[]{:S(2)}, u32[]{:S(2)}) %collective-permute-start.13) | collective-permute-done | bytes 32800 | tf_op jit(solution)/shard_map/ppermute | solution.py:40
  330.4 1.0 copy.79
  332.9 38.0 %all-to-all-done.2 = f32[1152,1,512]{2,1,0:T(1,128)S(1)} async-done(((f32[1152,1,512]{2,1,0:T(1,128)}), f32[1152,1,512]{2,1,0:T(1,128)S(1)}, u32[]{:S(2)}, u32[]{:S(2)}) %all-to-all-start.2) | async-done | bytes 2359328 | tf_op jit(solution)/shard_map/all_to_all | solution.py:221
  370.9 1.9 copy.77
  372.7 3.4 reshape.248
  (142 shorter events, 22.3 us)
Async XLA Ops:
  0.6 41.8 %copy-start = (f32[32]{0:T(128)S(1)}, f32[32]{0:T(128)}, u32[]{:S(2)}) copy-start(f32[32]{0:T(128)} %param.10) | copy-start | bytes 388
  2.4 51.0 %all-to-all-start = ((f32[64,1,1024]{2,1,0:T(1,128)}), f32[64,1,1024]{2,1,0:T(1,128)}, u32[]{:S(2)}, u32[]{:S(2)}) async-start(f32[64,1,1024]{2,1,0:T(1,128)} %reshape.282), calls=%async_computation | async-start | bytes 524288 | tf_op jit(solution)/shard_map/all_to_all | solution.py:47
  17.4 0.8 copy-start.5
  18.2 14.0 %copy-start.26 = (s32[64]{0:T(128)S(1)}, s32[64]{0:T(128)}, u32[]{:S(2)}) copy-start(s32[64]{0:T(128)} %param.15) | copy-start | bytes 772
  22.4 28.4 %collective-permute-start.2 = (f32[2,8,4096]{2,1,0:T(8,128)}, f32[2,8,4096]{2,1,0:T(8,128)}, u32[]{:S(2)}, u32[]{:S(2)}) collective-permute-start(f32[2,8,4096]{2,1,0:T(8,128)} %pad_maximum_fusion.9), channel_id=1, source_target_pairs={{0,4},{4,0},{8,12},{12,8},{16,20},{20,16},{24,28},{28,24},{32,36},... | collective-permute-start | bytes 786440 | tf_op jit(solution)/shard_map/ppermute | solution.py:29
  24.3 46.7 %collective-permute-start = (f32[18,1,4096]{2,0,1:T(8,128)}, f32[18,1,4096]{2,0,1:T(8,128)}, u32[]{:S(2)}, u32[]{:S(2)}) collective-permute-start(f32[18,1,4096]{2,0,1:T(8,128)} %get-tuple-element.50), channel_id=1, source_target_pairs={{0,1},{1,2},{2,3},{4,5},{5,6},{6,7},{8,9},{9,10},{10,11},{12,13},{... | collective-permute-start | bytes 884744 | tf_op jit(solution)/shard_map/ppermute | solution.py:39
  30.0 41.0 %collective-permute-start.1 = (f32[18,1,4096]{2,0,1:T(8,128)}, f32[18,1,4096]{2,0,1:T(8,128)}, u32[]{:S(2)}, u32[]{:S(2)}) collective-permute-start(f32[18,1,4096]{2,0,1:T(8,128)} %get-tuple-element.51), channel_id=1, source_target_pairs={{1,0},{2,1},{3,2},{5,4},{6,5},{7,6},{9,8},{10,9},{11,10},{13,12},{... | collective-permute-start | bytes 884744 | tf_op jit(solution)/shard_map/ppermute | solution.py:40
  39.2 4.6 %copy-start.24 = (f32[8,32]{1,0:T(8,128)S(1)}, f32[8,32]{1,0:T(8,128)}, u32[]{:S(2)}) copy-start(f32[8,32]{1,0:T(8,128)} %param.11) | copy-start | bytes 3076
  84.6 16.3 %copy-start.8 = (f32[8,4096]{1,0:T(8,128)S(1)}, f32[8,4096]{1,0:T(8,128)}, u32[]{:S(2)}) copy-start(f32[8,4096]{1,0:T(8,128)} %get-tuple-element.60) | copy-start | bytes 393220
  84.6 16.3 %copy-start.9 = (f32[8,4096]{1,0:T(8,128)S(1)}, f32[8,4096]{1,0:T(8,128)}, u32[]{:S(2)}) copy-start(f32[8,4096]{1,0:T(8,128)} %get-tuple-element.61) | copy-start | bytes 393220
  84.6 16.3 %copy-start.10 = (f32[8,4096]{1,0:T(8,128)S(1)}, f32[8,4096]{1,0:T(8,128)}, u32[]{:S(2)}) copy-start(f32[8,4096]{1,0:T(8,128)} %get-tuple-element.62) | copy-start | bytes 393220
  84.6 16.3 %copy-start.11 = (f32[8,4096]{1,0:T(8,128)S(1)}, f32[8,4096]{1,0:T(8,128)}, u32[]{:S(2)}) copy-start(f32[8,4096]{1,0:T(8,128)} %get-tuple-element.63) | copy-start | bytes 393220
  84.6 16.3 %copy-start.12 = (f32[8,4096]{1,0:T(8,128)S(1)}, f32[8,4096]{1,0:T(8,128)}, u32[]{:S(2)}) copy-start(f32[8,4096]{1,0:T(8,128)} %get-tuple-element.64) | copy-start | bytes 393220
  84.6 16.3 %copy-start.13 = (f32[8,4096]{1,0:T(8,128)S(1)}, f32[8,4096]{1,0:T(8,128)}, u32[]{:S(2)}) copy-start(f32[8,4096]{1,0:T(8,128)} %get-tuple-element.65) | copy-start | bytes 393220
  84.6 16.3 %copy-start.14 = (f32[8,4096]{1,0:T(8,128)S(1)}, f32[8,4096]{1,0:T(8,128)}, u32[]{:S(2)}) copy-start(f32[8,4096]{1,0:T(8,128)} %mul.423) | copy-start | bytes 393220
  84.7 16.3 %copy-start.15 = (f32[8,4096]{1,0:T(8,128)S(1)}, f32[8,4096]{1,0:T(8,128)}, u32[]{:S(2)}) copy-start(f32[8,4096]{1,0:T(8,128)} %mul.428) | copy-start | bytes 393220
  84.7 16.3 %copy-start.17 = (f32[18]{0:T(128)S(1)}, f32[18]{0:T(128)}, u32[]{:S(2)}) copy-start(f32[18]{0:T(128)} %get-tuple-element.8) | copy-start | bytes 220
  84.7 16.3 %copy-start.18 = (f32[18]{0:T(128)S(1)}, f32[18]{0:T(128)}, u32[]{:S(2)}) copy-start(f32[18]{0:T(128)} %get-tuple-element.9) | copy-start | bytes 220
  84.7 16.3 %copy-start.19 = (f32[18]{0:T(128)S(1)}, f32[18]{0:T(128)}, u32[]{:S(2)}) copy-start(f32[18]{0:T(128)} %get-tuple-element.10) | copy-start | bytes 220
  84.7 16.3 %copy-start.20 = (f32[18]{0:T(128)S(1)}, f32[18]{0:T(128)}, u32[]{:S(2)}) copy-start(f32[18]{0:T(128)} %get-tuple-element.11) | copy-start | bytes 220
  84.7 16.3 %copy-start.21 = (f32[18]{0:T(128)S(1)}, f32[18]{0:T(128)}, u32[]{:S(2)}) copy-start(f32[18]{0:T(128)} %get-tuple-element.78) | copy-start | bytes 220
  84.7 16.3 %copy-start.22 = (f32[18]{0:T(128)S(1)}, f32[18]{0:T(128)}, u32[]{:S(2)}) copy-start(f32[18]{0:T(128)} %get-tuple-element.79) | copy-start | bytes 220
  84.7 16.3 %copy-start.23 = (f32[18]{0:T(128)S(1)}, f32[18]{0:T(128)}, u32[]{:S(2)}) copy-start(f32[18]{0:T(128)} %get-tuple-element.82) | copy-start | bytes 220
  84.9 7.6 %collective-permute-start.5 = (f32[2,8,4096]{2,1,0:T(8,128)S(1)}, f32[2,8,4096]{2,1,0:T(8,128)S(1)}, u32[]{:S(2)}, u32[]{:S(2)}) collective-permute-start(f32[2,8,4096]{2,1,0:T(8,128)S(1)} %pad_maximum_fusion.10), channel_id=1, source_target_pairs={{0,4},{4,0},{8,12},{12,8},{16,20},{20,16},{24,28},{28,24},{32,36},... | collective-permute-start | bytes 786440 | tf_op jit(solution)/shard_map/ppermute | solution.py:29
  85.1 9.9 %collective-permute-start.3 = (f32[18,1,4096]{2,0,1:T(8,128)S(1)}, f32[18,1,4096]{2,0,1:T(8,128)S(1)}, u32[]{:S(2)}, u32[]{:S(2)}) collective-permute-start(f32[18,1,4096]{2,0,1:T(8,128)S(1)} %get-tuple-element.40), channel_id=1, source_target_pairs={{0,1},{1,2},{2,3},{4,5},{5,6},{6,7},{8,9},{9,10},{10,11},{12,13},{... | collective-permute-start | bytes 884744 | tf_op jit(solution)/shard_map/ppermute | solution.py:39
  90.3 10.6 %collective-permute-start.4 = (f32[18,1,4096]{2,0,1:T(8,128)S(1)}, f32[18,1,4096]{2,0,1:T(8,128)S(1)}, u32[]{:S(2)}, u32[]{:S(2)}) collective-permute-start(f32[18,1,4096]{2,0,1:T(8,128)S(1)} %get-tuple-element.41), channel_id=1, source_target_pairs={{1,0},{2,1},{3,2},{5,4},{6,5},{7,6},{9,8},{10,9},{11,10},{13,12},{... | collective-permute-start | bytes 884744 | tf_op jit(solution)/shard_map/ppermute | solution.py:40
  111.6 5.4 %collective-permute-start.8 = (f32[2,8,4096]{2,1,0:T(8,128)S(1)}, f32[2,8,4096]{2,1,0:T(8,128)S(1)}, u32[]{:S(2)}, u32[]{:S(2)}) collective-permute-start(f32[2,8,4096]{2,1,0:T(8,128)S(1)} %pad_maximum_fusion.11), channel_id=1, source_target_pairs={{0,4},{4,0},{8,12},{12,8},{16,20},{20,16},{24,28},{28,24},{32,36},... | collective-permute-start | bytes 786440 | tf_op jit(solution)/shard_map/ppermute | solution.py:29
  112.3 7.5 %collective-permute-start.6 = (f32[18,1,4096]{2,0,1:T(8,128)S(1)}, f32[18,1,4096]{2,0,1:T(8,128)S(1)}, u32[]{:S(2)}, u32[]{:S(2)}) collective-permute-start(f32[18,1,4096]{2,0,1:T(8,128)S(1)} %get-tuple-element.30), channel_id=1, source_target_pairs={{0,1},{1,2},{2,3},{4,5},{5,6},{6,7},{8,9},{9,10},{10,11},{12,13},{... | collective-permute-start | bytes 884744 | tf_op jit(solution)/shard_map/ppermute | solution.py:39
  114.9 10.6 %collective-permute-start.7 = (f32[18,1,4096]{2,0,1:T(8,128)S(1)}, f32[18,1,4096]{2,0,1:T(8,128)S(1)}, u32[]{:S(2)}, u32[]{:S(2)}) collective-permute-start(f32[18,1,4096]{2,0,1:T(8,128)S(1)} %get-tuple-element.31), channel_id=1, source_target_pairs={{1,0},{2,1},{3,2},{5,4},{6,5},{7,6},{9,8},{10,9},{11,10},{13,12},{... | collective-permute-start | bytes 884744 | tf_op jit(solution)/shard_map/ppermute | solution.py:40
  136.0 5.3 %collective-permute-start.11 = (f32[2,8,4096]{2,1,0:T(8,128)S(1)}, f32[2,8,4096]{2,1,0:T(8,128)S(1)}, u32[]{:S(2)}, u32[]{:S(2)}) collective-permute-start(f32[2,8,4096]{2,1,0:T(8,128)S(1)} %pad_maximum_fusion.12), channel_id=1, source_target_pairs={{0,4},{4,0},{8,12},{12,8},{16,20},{20,16},{24,28},{28,24},{32,36},... | collective-permute-start | bytes 786440 | tf_op jit(solution)/shard_map/ppermute | solution.py:29
  136.2 7.5 %collective-permute-start.9 = (f32[18,1,4096]{2,0,1:T(8,128)S(1)}, f32[18,1,4096]{2,0,1:T(8,128)S(1)}, u32[]{:S(2)}, u32[]{:S(2)}) collective-permute-start(f32[18,1,4096]{2,0,1:T(8,128)S(1)} %get-tuple-element.20), channel_id=1, source_target_pairs={{0,1},{1,2},{2,3},{4,5},{5,6},{6,7},{8,9},{9,10},{10,11},{12,13},{... | collective-permute-start | bytes 884744 | tf_op jit(solution)/shard_map/ppermute | solution.py:39
  138.9 10.6 %collective-permute-start.10 = (f32[18,1,4096]{2,0,1:T(8,128)S(1)}, f32[18,1,4096]{2,0,1:T(8,128)S(1)}, u32[]{:S(2)}, u32[]{:S(2)}) collective-permute-start(f32[18,1,4096]{2,0,1:T(8,128)S(1)} %get-tuple-element.21), channel_id=1, source_target_pairs={{1,0},{2,1},{3,2},{5,4},{6,5},{7,6},{9,8},{10,9},{11,10},{13,12},{... | collective-permute-start | bytes 884744 | tf_op jit(solution)/shard_map/ppermute | solution.py:40
  165.3 78.2 %all-to-all-start.1 = ((f32[18,64,512]{2,0,1:T(8,128)}), f32[18,64,512]{2,0,1:T(8,128)S(1)}, u32[]{:S(2)}, u32[]{:S(2)}) async-start(f32[18,64,512]{2,0,1:T(8,128)} %copy.73), calls=%async_computation.1 | async-start | bytes 6291456 | tf_op jit(solution)/shard_map/all_to_all | solution.py:219
  247.6 14.7 %copy-start.2 = (f32[1152,512]{1,0:T(8,128)S(1)}, f32[1152,512]{1,0:T(8,128)}, u32[]{:S(2)}) copy-start(f32[1152,512]{1,0:T(8,128)} %reshape.246) | copy-start | bytes 7077892
  262.2 22.9 %copy-start.3 = (f32[512,1152]{1,0:T(8,128)}, f32[512,1152]{1,0:T(8,128)S(1)}, u32[]{:S(2)}) copy-start(f32[512,1152]{1,0:T(8,128)S(1)} %fusion.128) | copy-start | bytes 7077892
  285.1 2.4 copy-start.4
  288.2 17.2 %all-to-all-start.3 = ((f32[64,2,1,512]{3,1,2,0:T(2,128)}), f32[64,2,1,512]{3,1,2,0:T(2,128)}, u32[]{:S(2)}, u32[]{:S(2)}) async-start(f32[64,2,1,512]{3,1,2,0:T(2,128)} %broadcast_in_dim.73), calls=%async_computation.3 | async-start | bytes 524288 | tf_op jit(solution)/shard_map/all_to_all | solution.py:47
  305.4 10.7 %copy-start.27 = (s32[64]{0:T(128)S(1)}, s32[64]{0:T(128)}, u32[]{:S(2)}) copy-start(s32[64]{0:T(128)} %param.15) | copy-start | bytes 772
  305.4 12.0 %copy-start.25 = (pred[64]{0:T(512)(128)(4,1)S(1)}, pred[64]{0:T(512)(128)(4,1)}, u32[]{:S(2)}) copy-start(pred[64]{0:T(512)(128)(4,1)} %compare_and_fusion) | copy-start | bytes 196
  305.4 12.2 %copy-start.6 = (f32[32,4096]{1,0:T(8,128)S(1)}, f32[32,4096]{1,0:T(8,128)}, u32[]{:S(2)}) copy-start(f32[32,4096]{1,0:T(8,128)} %copy-done.5) | copy-start | bytes 1572868
  305.4 14.9 %copy-start.7 = (f32[64,2,8,64]{3,2,1,0:T(8,128)S(1)}, f32[64,2,8,64]{3,2,1,0:T(8,128)}, u32[]{:S(2)}) copy-start(f32[64,2,8,64]{3,2,1,0:T(8,128)} %gather_fusion.1) | copy-start | bytes 786436
  305.5 65.4 %all-to-all-start.2 = ((f32[1152,1,512]{2,1,0:T(1,128)}), f32[1152,1,512]{2,1,0:T(1,128)S(1)}, u32[]{:S(2)}, u32[]{:S(2)}) async-start(f32[1152,1,512]{2,1,0:T(1,128)} %copy.76), calls=%async_computation.2 | async-start | bytes 4718592 | tf_op jit(solution)/shard_map/all_to_all | solution.py:221
  319.5 0.7 copy-start.16
  320.7 4.4 %collective-permute-start.12 = (f32[2,1,4096]{2,1,0:T(1,128)S(1)}, f32[2,1,4096]{2,1,0:T(1,128)S(1)}, u32[]{:S(2)}, u32[]{:S(2)}) collective-permute-start(f32[2,1,4096]{2,1,0:T(1,128)S(1)} %get-tuple-element.68), channel_id=1, source_target_pairs={{0,1},{1,2},{2,3},{4,5},{5,6},{6,7},{8,9},{9,10},{10,11},{12,13},{... | collective-permute-start | bytes 98312 | tf_op jit(solution)/shard_map/ppermute | solution.py:39
  322.7 7.0 %collective-permute-start.13 = (f32[2,1,4096]{2,1,0:T(1,128)S(1)}, f32[2,1,4096]{2,1,0:T(1,128)S(1)}, u32[]{:S(2)}, u32[]{:S(2)}) collective-permute-start(f32[2,1,4096]{2,1,0:T(1,128)S(1)} %get-tuple-element.69), channel_id=1, source_target_pairs={{1,0},{2,1},{3,2},{5,4},{6,5},{7,6},{9,8},{10,9},{11,10},{13,12},{... | collective-permute-start | bytes 98312 | tf_op jit(solution)/shard_map/ppermute | solution.py:40
  370.9 5.2 %copy-start.1 = (f32[32]{0:T(128)S(1)}, f32[32]{0:T(128)}, u32[]{:S(2)}) copy-start(f32[32]{0:T(128)} %param.10) | copy-start | bytes 388
where the time goes:
time: 381 us; the launch traced here: 376 us
  waiting for transfers between devices  135 us (35%)
  starting transfers between devices  71.5 us (19%)
  local copies, waits for them, and re-layouts  66.8 us (18%)
  other arithmetic  60.7 us (16%)
  matrix products  39.8 us (10%)
    all_to_all x1, waiting for transfers between devices, local(): lax.all_to_all(blocked, 'comp', split_axis=1, concat_axis=0, tiled=True)  67.8 us
    all_to_all x1, waiting for transfers between devices, local(): lax.all_to_all(updated, 'comp', split_axis=0, concat_axis=1, tiled=True)  38 us
    mul x4, other arithmetic, advance(): return ocean_rows[None] * (centre - change)  35.8 us
    dot_general x1, matrix products, source_local(): jnp.dot(interp, flat_spec, precision=HIGHEST, preferred_element_type=jnp....  22.8 us
    ppermute x5, waiting for transfers between devices, padded_2(): after = lax.ppermute(first, axis, down)  22 us
    all_to_all x2, starting transfers between devices, from_everyone(): lax.all_to_all(jnp.broadcast_to(value[None], (count, *value.shape)), axis...  20.1 us
    ppermute x5, starting transfers between devices, padded_2(): before = lax.ppermute(last, axis, up)  18.2 us
    dot_general x1, matrix products, source_local(): lax.dot_general(interp, flat_spec, (((0,), (0,)), ((), ())), precision=HI...  14.6 us
  transfers between devices with their start and end apart: 18, of which 11 were waited for; matrix products, arithmetic and copies ran while one was open for 17% of the time, Pallas kernels for 0%

commit v1 on v0

v1 whole, which is shorter than its diff:
```python
import math

import jax
import jax.numpy as jnp
import numpy as np
from jax import lax
from jax.experimental import pallas as pl
from jax.experimental.pallas import tpu as pltpu
from jax.sharding import PartitionSpec as P

DIRS = 36
FREQ = 32
CLASSES = 8
SUBSTEPS = 4
COMPS = 1152
OWN = 18
ROWS = 8
TOTAL_ROWS = 32
LON = 4096
TILES = 64
PLANE = 8
LANES = 128
BLOCK = OWN * 4
CHUNK = 144
POINTS = 512
PIECE = 1024
MESH = pl.DeviceIdType.MESH
f32 = jnp.float32
bf16 = jnp.bfloat16


def plane_offset(step):
    return 4 + (1 - 2 * (step % 2)) * ((step + 1) // 2)


def wave_kernel(
    spectrum, cat, sea, classes, interp_any, weights, courant, refraction, inverse, cosine, sine,
    recv2, drift_all, gathered, beside,
    state, rows_out, rows_in, base_u, base_v, turning, ocean, send1, recv1, interp, interp_t, split,
    points, points_hi, points_lo, drift_block,
    interp_sem, cur_send, cur_recv, beside_send, beside_recv, edge_send, edge_recv,
    in_send, in_recv, out_send, out_recv, drift_send, drift_recv, own_sem,
):
    me = lax.axis_index("comp")
    band = lax.axis_index("band")
    plane = me // PLANE
    low = me % PLANE
    partner = me + 1 - 2 * (me % 2)
    freq = me // 2
    first_dir = (me % 2) * OWN
    south = band > 0
    north = band < 3

    load_interp = pltpu.make_async_copy(interp_any, interp, interp_sem)
    load_interp.start()

    barrier = pltpu.get_barrier_semaphore()

    @pl.loop(1, TILES)
    def _(t):
        pl.semaphore_signal(barrier, inc=1, device_id={"comp": (me + t) % TILES}, device_id_type=MESH)

    @pl.when(south)
    def _():
        pl.semaphore_signal(barrier, inc=1, device_id={"band": band - 1}, device_id_type=MESH)

    @pl.when(north)
    def _():
        pl.semaphore_signal(barrier, inc=1, device_id={"band": band + 1}, device_id_type=MESH)

    rows8 = pl.ds(pl.multiple_of(band * ROWS, ROWS), ROWS)
    ocean[...] = sea[rows8, :].astype(f32)

    def row_copy(side, step):
        return pltpu.make_async_remote_copy(
            src_ref=rows_out.at[step, side],
            dst_ref=rows_in.at[step, side],
            send_sem=edge_send.at[step, side],
            recv_sem=edge_recv.at[step, side],
            device_id={"band": band + 1 - 2 * side},
            device_id_type=MESH,
        )

    def dir_copy(side, step):
        return pltpu.make_async_remote_copy(
            src_ref=state.at[step, OWN if side == 0 else 1],
            dst_ref=state.at[step, 0 if side == 0 else OWN + 1],
            send_sem=edge_send.at[step, 2 + side],
            recv_sem=edge_recv.at[step, 2 + side],
            device_id={"comp": partner},
            device_id_type=MESH,
        )

    def start_edges(step):
        dir_copy(0, step).start()
        dir_copy(1, step).start()

        @pl.when(north)
        def _():
            row_copy(0, step).start()

        @pl.when(south)
        def _():
            row_copy(1, step).start()

    def finish_edges(step):
        for side in range(2):
            dir_copy(side, step).wait_recv()
            dir_copy(side, step).wait_send()

        @pl.when(south)
        def _():
            row_copy(0, step).wait_recv()
            row_copy(1, step).wait_send()

        @pl.when(north)
        def _():
            row_copy(1, step).wait_recv()
            row_copy(0, step).wait_send()

    @pl.loop(0, OWN)
    def _(i):
        masked = spectrum[i] * ocean[...]
        state[0, i + 1] = masked
        rows_out[0, 0, i] = masked[ROWS - 1 :, :]
        rows_out[0, 1, i] = masked[:1, :]

    pl.semaphore_wait(barrier, TILES - 1 + jnp.where(south, 1, 0) + jnp.where(north, 1, 0))

    def cur_copy(t):
        return pltpu.make_async_remote_copy(
            src_ref=cat,
            dst_ref=gathered.at[me],
            send_sem=cur_send.at[t],
            recv_sem=cur_recv.at[t],
            device_id={"comp": (me + t) % TILES},
            device_id_type=MESH,
        )

    def beside_copy(side):
        return pltpu.make_async_remote_copy(
            src_ref=cat,
            dst_ref=beside.at[side],
            send_sem=beside_send.at[side],
            recv_sem=beside_recv.at[side],
            device_id={"band": band + 1 - 2 * side},
            device_id_type=MESH,
        )

    @pl.loop(1, TILES)
    def _(t):
        cur_copy(t).start()

    start_edges(0)

    @pl.when(north)
    def _():
        beside_copy(0).start()

    @pl.when(south)
    def _():
        beside_copy(1).start()

    gathered[me] = cat[...]

    @pl.when(band == 0)
    def _():
        rows_in[:, 0] = jnp.zeros((SUBSTEPS, OWN, 1, LON), f32)

    @pl.when(band == 3)
    def _():
        rows_in[:, 1] = jnp.zeros((SUBSTEPS, OWN, 1, LON), f32)

    own_class = classes[rows8, :]
    turned = jnp.zeros((ROWS, LON), f32)
    for level in range(CLASSES):
        turned = jnp.where(own_class == level, refraction[level, freq], turned)
    turning[...] = turned

    @pl.loop(1, TILES)
    def _(t):
        cur_copy(t).wait_recv()

    lane = lax.broadcasted_iota(jnp.int32, (ROWS, LANES), 1)
    for u in range(TILES // 2):
        one = gathered[inverse[2 * u]]
        two = gathered[inverse[2 * u + 1]]
        at = slice(u * LANES, (u + 1) * LANES)
        base_u[:, at] = 0.025 * jnp.where(lane < 64, one, pltpu.roll(two, 64, 1))
        base_v[:, at] = 0.025 * jnp.where(lane < 64, pltpu.roll(one, 64, 1), two)

    row = lax.broadcasted_iota(jnp.int32, (ROWS, PIECE), 0)
    speed = courant[freq]

    def advanced(step, i, piece):
        lo = piece * PIECE
        at = slice(lo, lo + PIECE)
        centre = state[step, i + 1, :, at]
        if piece == 0:
            west_piece = state[step, i + 1, :, LON - LANES :]
        else:
            west_piece = state[step, i + 1, :, lo - LANES : lo]
        if piece == LON // PIECE - 1:
            east_piece = state[step, i + 1, :, :LANES]
        else:
            east_piece = state[step, i + 1, :, lo + PIECE : lo + PIECE + LANES]
        wide = jnp.concatenate([west_piece, centre, east_piece], axis=1)
        west = pltpu.roll(wide, 1, 1)[:, LANES:-LANES]
        east = pltpu.roll(wide, PIECE + 2 * LANES - 1, 1)[:, LANES:-LANES]
        below = jnp.where(row == 0, rows_in[step, 0, i, :, at], pltpu.roll(centre, 1, 0))
        above = jnp.where(row == ROWS - 1, rows_in[step, 1, i, :, at], pltpu.roll(centre, ROWS - 1, 0))
        before = state[step, i, :, at]
        after = state[step, i + 2, :, at]
        cos_d = cosine[first_dir + i]
        ax = base_u[:, at] + speed * cos_d
        ay = base_v[:, at] + speed * sine[first_dir + i]
        turn = turning[:, at] * cos_d
        change = (
            jnp.maximum(ax, 0.0) * (centre - west) + jnp.minimum(ax, 0.0) * (east - centre)
            + (jnp.maximum(ay, 0.0) * (centre - below) + jnp.minimum(ay, 0.0) * (above - centre))
            + (jnp.maximum(turn, 0.0) * (centre - before) + jnp.minimum(turn, 0.0) * (after - centre))
        )
        return ocean[:, at] * (centre - change)

    for step in range(SUBSTEPS - 1):
        finish_edges(step)

        @pl.loop(0, OWN)
        def _(i):
            for piece in range(LON // PIECE):
                at = slice(piece * PIECE, (piece + 1) * PIECE)
                new = advanced(step, i, piece)
                state[step + 1, i + 1, :, at] = new
                rows_out[step + 1, 0, i, :, at] = new[ROWS - 1 :, :]
                rows_out[step + 1, 1, i, :, at] = new[:1, :]

        start_edges(step + 1)

    finish_edges(SUBSTEPS - 1)

    @pl.loop(0, OWN)
    def _(i):
        for piece in range(LON // PIECE):
            new = advanced(SUBSTEPS - 1, i, piece)
            for tile in range(PIECE // LANES):
                col = piece * (PIECE // LANES) + tile
                first = (col // 4) * ROWS * BLOCK + col % 4
                send1[pl.ds(first + i * 4, ROWS, stride=BLOCK), :] = new[:, tile * LANES : (tile + 1) * LANES]

    def block_of(ref, owner):
        return ref.at[pl.ds(pl.multiple_of(owner * BLOCK, 8), BLOCK)]

    def in_copy(k):
        to = ((plane + plane_offset(k // PLANE)) % PLANE) * PLANE + (low + k % PLANE) % PLANE
        return pltpu.make_async_remote_copy(
            src_ref=block_of(send1, to),
            dst_ref=block_of(recv1, me),
            send_sem=in_send.at[k],
            recv_sem=in_recv.at[k],
            device_id={"comp": to},
            device_id_type=MESH,
        )

    @pl.loop(0, 56)
    def _(k):
        in_copy(k).start()

    @pl.loop(57, TILES)
    def _(k):
        in_copy(k).start()

    own_rows = pl.ds(pl.multiple_of(me * BLOCK, 8), BLOCK)
    recv1[own_rows, :] = send1[own_rows, :]

    load_interp.wait()

    @pl.loop(0, COMPS // LANES)
    def _(b):
        cols = pl.ds(pl.multiple_of(b * LANES, LANES), LANES)
        interp_t[cols, :] = interp[:, cols].T

    @pl.loop(0, COMPS // CHUNK)
    def _(c):
        rows = pl.ds(pl.multiple_of(c * CHUNK, 16), CHUNK)
        for part, source in enumerate((interp, interp_t)):
            value = source[rows, :]
            high = value.astype(bf16)
            split[c, part * CHUNK : (part + 1) * CHUNK, :] = high
            split[c, (2 + part) * CHUNK : (3 + part) * CHUNK, :] = (value - high.astype(f32)).astype(bf16)

    @pl.loop(0, 56)
    def _(k):
        in_copy(k).wait_recv()

    @pl.loop(57, TILES)
    def _(k):
        in_copy(k).wait_recv()

    @pl.loop(0, COMPS // CHUNK)
    def _(c):
        rows = pl.ds(pl.multiple_of(c * CHUNK, 16), CHUNK)
        for q in range(4):
            value = recv1[pl.ds(c * (CHUNK * 4) + q, CHUNK, stride=4), :]
            at = slice(q * LANES, (q + 1) * LANES)
            high = value.astype(bf16)
            points[rows, at] = value
            points_hi[rows, at] = high
            points_lo[rows, at] = (value - high.astype(f32)).astype(bf16)

    @pl.loop(0, 56)
    def _(k):
        in_copy(k).wait_send()

    @pl.loop(57, TILES)
    def _(k):
        in_copy(k).wait_send()

    def out_copy(to):
        return pltpu.make_async_remote_copy(
            src_ref=block_of(send1, to),
            dst_ref=block_of(recv2, me),
            send_sem=out_send.at[to],
            recv_sem=out_recv.at[me],
            device_id={"comp": to},
            device_id_type=MESH,
        )

    own_copy = pltpu.make_async_copy(block_of(send1, me), block_of(recv2, me), own_sem)

    def source_chunk(c, drift):
        group = (plane + plane_offset(c)) % PLANE
        rows = pl.ds(pl.multiple_of(group * CHUNK, 16), CHUNK)
        both = jnp.dot(split[group], points_hi[...], preferred_element_type=f32)
        more = jnp.dot(split[group, : 2 * CHUNK, :], points_lo[...], preferred_element_type=f32)
        sums = both[: 2 * CHUNK] + (both[2 * CHUNK :] + more)
        forward, backward = sums[:CHUNK], sums[CHUNK:]
        wave = points[rows, :]
        new = wave + 0.5 * (forward * backward - 0.5 * wave * (forward + backward))
        for q in range(4):
            send1[pl.ds(group * (CHUNK * 4) + q, CHUNK, stride=4), :] = new[:, q * LANES : (q + 1) * LANES]

        @pl.loop(0, PLANE)
        def _(e):
            to = group * PLANE + (low + e) % PLANE

            @pl.when(to != me)
            def _():
                out_copy(to).start()

        held = weights[rows, :]
        return tuple(
            drift[a] + jnp.sum((held[:, a : a + 1] * new).reshape(CHUNK // 8, 8, POINTS), axis=0) for a in range(2)
        )

    drift = lax.fori_loop(
        0, PLANE, source_chunk, (jnp.zeros((8, POINTS), f32), jnp.zeros((8, POINTS), f32))
    )
    own_copy.start()
    for a in range(2):
        total = jnp.sum(drift[a], axis=0, keepdims=True)
        for q in range(4):
            drift_block[a * 4 + q : a * 4 + q + 1, :] = total[:, q * LANES : (q + 1) * LANES]

    def drift_copy(t):
        return pltpu.make_async_remote_copy(
            src_ref=drift_block,
            dst_ref=drift_all.at[pl.ds(pl.multiple_of(me * 8, 8), 8)],
            send_sem=drift_send.at[t],
            recv_sem=drift_recv.at[t],
            device_id={"comp": (me + t) % TILES},
            device_id_type=MESH,
        )

    @pl.loop(1, TILES)
    def _(t):
        drift_copy(t).start()

    drift_all[pl.ds(pl.multiple_of(me * 8, 8), 8), :] = drift_block[...]

    @pl.loop(1, TILES)
    def _(t):
        other = (me + t) % TILES
        cur_copy(t).wait_send()
        out_copy(other).wait_send()
        pltpu.make_async_remote_copy(
            src_ref=block_of(send1, other),
            dst_ref=block_of(recv2, other),
            send_sem=out_send.at[other],
            recv_sem=out_recv.at[other],
            device_id={"comp": other},
            device_id_type=MESH,
        ).wait_recv()
        drift_copy(t).wait()

    own_copy.wait()

    @pl.when(north)
    def _():
        beside_copy(0).wait_send()
        beside_copy(1).wait_recv()

    @pl.when(south)
    def _():
        beside_copy(1).wait_send()
        beside_copy(0).wait_recv()


def finish_kernel(blocks, drift_all, gathered, beside, cat, sea, coriolis, owner, inverse, place, out, ocean_out):
    @pl.loop(0, OWN)
    def _(i):
        for col in range(LON // LANES):
            first = (col // 4) * ROWS * BLOCK + col % 4
            out[i, :, col * LANES : (col + 1) * LANES] = blocks[pl.ds(first + i * 4, ROWS, stride=BLOCK), :]

    me, band = place[0], place[1]
    tile = owner[me]
    lane = lax.broadcasted_iota(jnp.int32, (ROWS, LANES), 1)
    row = lax.broadcasted_iota(jnp.int32, (ROWS, LANES), 0)
    left = lane < 64

    def twice(value, half):
        other = pltpu.roll(value, 64, 1)
        mine = jnp.where(half == 0, value, other)
        return mine, jnp.where(half == 0, other, value)

    def mask(which_tile, which_band):
        rows = pl.ds(pl.multiple_of(which_band * ROWS, ROWS), ROWS)
        cols = pl.ds(pl.multiple_of((which_tile // 2) * LANES, LANES), LANES)
        at_left, at_right = twice(sea[rows, cols].astype(f32), which_tile % 2)
        return jnp.where(left, at_left, at_right)

    own = mask(tile, band)
    held = cat[...] * own
    west_tile, east_tile = (tile + TILES - 1) % TILES, (tile + 1) % TILES
    held_w = gathered[inverse[west_tile]] * mask(west_tile, band)
    held_e = gathered[inverse[east_tile]] * mask(east_tile, band)
    held_s = jnp.where(band > 0, beside[0] * mask(tile, jnp.maximum(band - 1, 0)), 0.0)
    held_n = jnp.where(band < 3, beside[1] * mask(tile, jnp.minimum(band + 1, 3)), 0.0)
    west = jnp.where(lane % 64 == 0, pltpu.roll(held_w, 65, 1), pltpu.roll(held, 1, 1))
    east = jnp.where(lane % 64 == 63, pltpu.roll(held_e, 63, 1), pltpu.roll(held, 127, 1))
    below = jnp.where(row == 0, pltpu.roll(held_s, 1, 0), pltpu.roll(held, 1, 0))
    above = jnp.where(row == ROWS - 1, pltpu.roll(held_n, 7, 0), pltpu.roll(held, 7, 0))
    lap = west + east + below + above - 4.0 * held
    first = (tile // 8) * 64 + (tile % 8) // 2
    eastward, _ = twice(drift_all[pl.ds(first, ROWS, stride=8), :], tile % 2)
    _, northward = twice(drift_all[pl.ds(first + 4, ROWS, stride=8), :], tile % 2)
    stokes = jnp.where(left, eastward, northward)
    rows8 = pl.ds(pl.multiple_of(band * ROWS, ROWS), ROWS)
    turn = jnp.where(left, 1.0, -1.0) * coriolis[rows8, :]
    other = pltpu.roll(held + stokes, 64, 1)
    ocean_out[...] = own * (held + 0.5 * (turn * other + 0.2 * lap - 0.1 * held))


def tables():
    angles = np.arange(DIRS, dtype=np.float32) * np.float32(2.0 * math.pi / DIRS)
    cosine, sine = np.cos(angles).astype(np.float32), np.sin(angles).astype(np.float32)
    k = np.arange(COMPS)
    scale = (np.float32(0.2) * (k // DIRS + 1).astype(np.float32) / np.float32(FREQ)).astype(np.float32)
    weights = np.stack([scale * cosine[k % DIRS], scale * sine[k % DIRS]], axis=1)
    latitude = -1.2 + 2.4 * (np.arange(TOTAL_ROWS, dtype=np.float32) + np.float32(0.5)) / TOTAL_ROWS
    coriolis = np.broadcast_to(np.sin(latitude.astype(np.float32))[:, None], (TOTAL_ROWS, LANES))
    return cosine, sine, weights.astype(np.float32), coriolis.astype(np.float32)


def local(spectrum, currents, group_courant, refraction, interp, sea_mask, depth_class, owner_map):
    cosine, sine, weights, coriolis = tables()
    cat = jnp.concatenate([currents[0], currents[1]], axis=1)
    index = jnp.arange(TILES, dtype=jnp.int32)
    inverse = jnp.sum(jnp.where(owner_map[None, :] == index[:, None], index[None, :], 0), axis=1)
    place = jnp.stack([lax.axis_index("comp"), lax.axis_index("band")]).astype(jnp.int32)
    vmem, smem = pl.BlockSpec(memory_space=pltpu.VMEM), pl.BlockSpec(memory_space=pltpu.SMEM)
    anywhere = pl.BlockSpec(memory_space=pl.ANY)
    dma = pltpu.SemaphoreType.DMA
    wide = (ROWS, LON)
    blocks, drift_all, gathered, beside = pl.pallas_call(
        wave_kernel,
        out_shape=(
            jax.ShapeDtypeStruct((TILES * BLOCK, LANES), f32),
            jax.ShapeDtypeStruct((TILES * 8, LANES), f32),
            jax.ShapeDtypeStruct((TILES, ROWS, LANES), f32),
            jax.ShapeDtypeStruct((2, ROWS, LANES), f32),
        ),
        in_specs=[vmem, vmem, vmem, vmem, anywhere, vmem, smem, smem, smem, smem, smem],
        out_specs=(anywhere, vmem, vmem, vmem),
        scratch_shapes=[
            pltpu.VMEM((SUBSTEPS, OWN + 2, ROWS, LON), f32),
            pltpu.VMEM((SUBSTEPS, 2, OWN, 1, LON), f32),
            pltpu.VMEM((SUBSTEPS, 2, OWN, 1, LON), f32),
            pltpu.VMEM(wide, f32),
            pltpu.VMEM(wide, f32),
            pltpu.VMEM(wide, f32),
            pltpu.VMEM(wide, f32),
            pltpu.VMEM((TILES * BLOCK, LANES), f32),
            pltpu.VMEM((TILES * BLOCK, LANES), f32),
            pltpu.VMEM((COMPS, COMPS), f32),
            pltpu.VMEM((COMPS, COMPS), f32),
            pltpu.VMEM((COMPS // CHUNK, 4 * CHUNK, COMPS), bf16),
            pltpu.VMEM((COMPS, POINTS), f32),
            pltpu.VMEM((COMPS, POINTS), bf16),
            pltpu.VMEM((COMPS, POINTS), bf16),
            pltpu.VMEM((8, LANES), f32),
            dma,
            dma((TILES,)),
            dma((TILES,)),
            dma((2,)),
            dma((2,)),
            dma((SUBSTEPS, 4)),
            dma((SUBSTEPS, 4)),
            dma((TILES,)),
            dma((TILES,)),
            dma((TILES,)),
            dma((TILES,)),
            dma((TILES,)),
            dma((TILES,)),
            dma,
        ],
        compiler_params=pltpu.CompilerParams(
            collective_id=0, has_side_effects=True, vmem_limit_bytes=60 * 2**20
        ),
        name="waves",
    )(
        spectrum, cat, sea_mask, depth_class, interp, jnp.asarray(weights), group_courant, refraction, inverse,
        jnp.asarray(cosine), jnp.asarray(sine),
    )
    out, ocean_cat = pl.pallas_call(
        finish_kernel,
        out_shape=(
            jax.ShapeDtypeStruct((OWN, ROWS, LON), f32),
            jax.ShapeDtypeStruct((ROWS, LANES), f32),
        ),
        in_specs=[vmem] * 7 + [smem] * 3,
        out_specs=(vmem, vmem),
        compiler_params=pltpu.CompilerParams(vmem_limit_bytes=32 * 2**20),
        name="finish",
    )(
        blocks, drift_all, gathered, beside, cat, sea_mask, jnp.asarray(coriolis), owner_map, inverse, place,
    )
    ocean_out = jnp.stack([ocean_cat[:, :64], ocean_cat[:, 64:]])
    return out, ocean_out


def solution(mesh):
    in_specs = (P("comp", "band", None), P(None, "band", "comp"), P(), P(), P(), P(), P(), P())
    out_specs = (P("comp", "band", None), P(None, "band", "comp"))
    return jax.shard_map(local, mesh=mesh, in_specs=in_specs, out_specs=out_specs, check_vma=False)
```

time: 381 us -> 202 us (0.53); the launches traced: 376 us -> 202 us
  Pallas kernels: 0 us -> 193 us
  waiting for transfers between devices: 135 us -> 0 us
  starting transfers between devices: 71.5 us -> 0 us
  local copies, waits for them, and re-layouts: 66.8 us -> 5.05 us
  other arithmetic: 60.7 us -> 2.63 us
  matrix products: 39.8 us -> 0 us
    pallas_call x0 -> x2, Pallas kernels: none -> 193 us  [the longest x1 191 us: local(): pl.pallas_call(wave_kernel, out_shape=(jax.ShapeDtypeStruct((TILES * BLOC...]
    all_to_all x4 -> x0, waiting for transfers between devices: 106 us -> none  [the longest x1 67.8 us: local(): lax.all_to_all(blocked, 'comp', split_axis=1, concat_axis=0, tiled=True)]
    all_to_all x4 -> x0, starting transfers between devices: 41 us -> none  [the longest x2 20.1 us: from_everyone(): lax.all_to_all(jnp.broadcast_to(value[None], (count, *value.shape)), axis...]
    mul x9 -> x0, other arithmetic: 40.5 us -> none  [the longest x4 35.8 us: advance(): return ocean_rows[None] * (centre - change)]
    dot_general x3 -> x0, matrix products: 39.8 us -> none  [the longest x1 22.8 us: source_local(): jnp.dot(interp, flat_spec, precision=HIGHEST, preferred_element_type=jnp....]
    ppermute x14 -> x0, starting transfers between devices: 30.6 us -> none  [the longest x5 18.2 us: padded_2(): before = lax.ppermute(last, axis, up)]
    ppermute x14 -> x0, waiting for transfers between devices: 29.2 us -> none  [the longest x5 22 us: padded_2(): after = lax.ppermute(first, axis, down)]
    slice x44 -> x0, local copies, waits for them, and re-layouts: 20.8 us -> none  [the longest x8 8.24 us: advance(): east_cols = jnp.roll(centre, -1, axis=2)]
  transfers between devices with their start and end apart: 18 -> 0, of which waited for: 11 -> 0; matrix products, arithmetic and copies ran while one was open for 17% -> 0% of each run, Pallas kernels for 0% -> 0%
where the time goes in v1:
time: 202 us
  Pallas kernels  193 us (96%)
  local copies, waits for them, and re-layouts  5.05 us (2%)
  other arithmetic  2.63 us (1%)
    pallas_call x1, Pallas kernels, local(): pl.pallas_call(wave_kernel, out_shape=(jax.ShapeDtypeStruct((TILES * BLOC...  191 us
    unnamed x18, local copies, waits for them, and re-layouts  4.27 us

profile of v1, /device:TPU:1, one launch (start us, length us, event | category | flops | bytes accessed | tf_op | source)
XLA Modules:
  0.0 201.9 jit_solution(7855213514140942376)
XLA Ops:
  0.6 0.1 pad_add_fusion.place
  0.7 1.3 select_reduce_fusion.inverse
  2.0 0.7 slice_bitcast_fusion.3
  2.7 0.7 pad_maximum_fusion.1.cat
  3.4 0.0 copy-start.1
  3.4 0.0 copy-start.4
  3.4 0.0 copy-start.5
  3.4 0.0 copy-start.7
  3.4 0.0 copy-start.8
  3.4 191.0 %waves.1 = (f32[4608,128]{1,0:T(8,128)}, f32[512,128]{1,0:T(8,128)}, f32[64,8,128]{2,1,0:T(8,128)}, f32[2,8,128]{2,1,0:T(8,128)}) custom-call(f32[18,8,4096]{2,1,0:T(8,128)} %spectrum.1, f32[8,128]{1,0:T(8,128)} %pad_maximum_fusion.1.cat, s32[32,4096]{1,0:T(8,128)} %sea.3, s32[32,4096]{1,0:T(8,128)} %classes.1, f32[1152,1152]{1,0:T(8,128)} %interp_any.1, ...), custom_call_target="tpu_custom_call" | custom-call | tf_op jit(solution)/shard_map/waves/pallas_call | solution.py:475
  194.4 0.0 copy-done.1
  194.4 0.0 copy-done.4
  194.4 0.0 copy-done.5
  194.4 0.0 copy-done.7
  194.4 0.0 copy-done.8
  194.4 0.0 copy-start
  194.4 1.7 copy-done
  196.1 0.0 copy-start.2
  196.1 0.9 copy-done.2
  197.1 0.0 copy-start.3
  197.1 0.9 copy-done.3
  198.0 0.0 copy-start.6
  198.0 0.7 copy-done.6
  198.7 2.5 %finish.1 = (f32[18,8,4096]{2,1,0:T(8,128)}, f32[8,128]{1,0:T(8,128)S(1)}) custom-call(f32[4608,128]{1,0:T(8,128)S(1)} %copy-done, f32[512,128]{1,0:T(8,128)S(1)} %copy-done.2, f32[64,8,128]{2,1,0:T(8,128)S(1)} %copy-done.3, f32[2,8,128]{2,1,0:T(8,128)S(1)} %copy-done.6, f32[8,128]{1,0:T(8,128)S(1)} %copy-done.4, s32[32,4096]{1,0:T(8,128)S(1)} %copy-done.1, ...), custom_call_target="tpu_custom_call" | custom-call | tf_op jit(solution)/shard_map/finish/pallas_call | solution.py:525
  201.2 0.1 slice_bitcast_fusion.1
  201.3 0.6 pad_maximum_fusion
Async XLA Ops:
  3.4 191.0 %copy-start.1 = (s32[32,4096]{1,0:T(8,128)S(1)}, s32[32,4096]{1,0:T(8,128)}, u32[]{:S(2)}) copy-start(s32[32,4096]{1,0:T(8,128)} %sea.3) | copy-start | bytes 1572868
  3.4 191.0 %copy-start.4 = (f32[8,128]{1,0:T(8,128)S(1)}, f32[8,128]{1,0:T(8,128)}, u32[]{:S(2)}) copy-start(f32[8,128]{1,0:T(8,128)} %pad_maximum_fusion.1.cat) | copy-start | bytes 12292
  3.4 191.0 %copy-start.5 = (f32[32,128]{1,0:T(8,128)S(1)}, f32[32,128]{1,0:T(8,128)}, u32[]{:S(2)}) copy-start(f32[32,128]{1,0:T(8,128)} %constant.22.clone.coriolis) | copy-start | bytes 49156
  3.4 191.0 %copy-start.7 = (s32[64]{0:T(128)S(1)}, s32[64]{0:T(128)}, u32[]{:S(2)}) copy-start(s32[64]{0:T(128)} %select_reduce_fusion.inverse) | copy-start | bytes 772
  3.4 191.1 %copy-start.8 = (s32[64]{0:T(128)S(1)}, s32[64]{0:T(128)}, u32[]{:S(2)}) copy-start(s32[64]{0:T(128)} %owner.1) | copy-start | bytes 772
  194.4 1.7 copy-start
  196.1 0.9 copy-start.2
  197.1 0.9 copy-start.3
  198.0 0.7 copy-start.6

commit v2 on v1

v2 whole, which is shorter than its diff:
```python
import math

import jax
import jax.numpy as jnp
import numpy as np
from jax import lax
from jax.experimental import pallas as pl
from jax.experimental.pallas import tpu as pltpu
from jax.sharding import PartitionSpec as P

DIRS = 36
FREQ = 32
CLASSES = 8
SUBSTEPS = 4
COMPS = 1152
OWN = 18
ROWS = 8
TOTAL_ROWS = 32
LON = 4096
TILES = 64
PLANE = 8
LANES = 128
BLOCK = OWN * 4
CHUNK = 144
POINTS = 512
HALF = 2048
REGION = HALF + 2 * LANES
PIECE = 1152
MESH = pl.DeviceIdType.MESH
f32 = jnp.float32
bf16 = jnp.bfloat16


def plane_offset(step):
    return 4 + (1 - 2 * (step % 2)) * ((step + 1) // 2)


def order_of(device):
    return (device // 2) % 2 * (TILES // 2) + device // 4 * 2 + device % 2


def block_of(ref, which):
    return ref.at[pl.ds(pl.multiple_of(which * BLOCK, 8), BLOCK)]


def wait_bytes(ref, sem):
    pltpu.make_async_copy(ref, ref, sem).wait()


def wave_kernel(
    spectrum, currents, sea, classes, interp_any, weights, coriolis, courant, refraction, owner, inverse, cosine, sine,
    out_any, ocean_out,
    state, rows_out, rows_in, base_u, base_v, turning, ocean, send1, recv1, send2, recv2, out, interp, split,
    points, points_hi, points_lo, cat, gathered, beside, drift_block, drift_all, masks,
    interp_sem, cur_send, cur_recv, beside_send, beside_recv, edge_send, edge_recv,
    in_send, in_recv, out_send, out_recv, drift_send, drift_recv, store_sem,
):
    me = lax.axis_index("comp")
    band = lax.axis_index("band")
    plane = me // PLANE
    low = me % PLANE
    partner = me + 1 - 2 * (me % 2)
    freq = me // 2
    first_dir = (me % 2) * OWN
    my_order = order_of(me)
    south = band > 0
    north = band < 3

    load_interp = pltpu.make_async_copy(interp_any, interp, interp_sem)
    load_interp.start()

    barrier = pltpu.get_barrier_semaphore()

    @pl.loop(1, TILES)
    def _(t):
        pl.semaphore_signal(barrier, inc=1, device_id={"comp": (me + t) % TILES}, device_id_type=MESH)

    @pl.when(south)
    def _():
        pl.semaphore_signal(barrier, inc=1, device_id={"band": band - 1}, device_id_type=MESH)

    @pl.when(north)
    def _():
        pl.semaphore_signal(barrier, inc=1, device_id={"band": band + 1}, device_id_type=MESH)

    rows8 = pl.ds(pl.multiple_of(band * ROWS, ROWS), ROWS)

    def store_wrapped(ref, value):
        ref[:, LANES : LANES + LON] = value
        ref[:, :LANES] = value[:, LON - LANES :]
        ref[:, LANES + LON :] = value[:, :LANES]

    store_wrapped(ocean, sea[rows8, :].astype(f32))
    cat[:, :64] = currents[0]
    cat[:, 64:] = currents[1]

    def row_copy(half, side, step):
        return pltpu.make_async_remote_copy(
            src_ref=rows_out.at[half, step, side],
            dst_ref=rows_in.at[half, step, side],
            send_sem=edge_send.at[half, step, side],
            recv_sem=edge_recv.at[half, step, side],
            device_id={"band": band + 1 - 2 * side},
            device_id_type=MESH,
        )

    def dir_copy(half, side, step):
        return pltpu.make_async_remote_copy(
            src_ref=state.at[half, step, OWN if side == 0 else 1],
            dst_ref=state.at[half, step, 0 if side == 0 else OWN + 1],
            send_sem=edge_send.at[half, step, 2 + side],
            recv_sem=edge_recv.at[half, step, 2 + side],
            device_id={"comp": partner},
            device_id_type=MESH,
        )

    def start_edges(half, step):
        @pl.when(north)
        def _():
            row_copy(half, 0, step).start()

        @pl.when(south)
        def _():
            row_copy(half, 1, step).start()

        dir_copy(half, 0, step).start()
        dir_copy(half, 1, step).start()

    def finish_edges(half, step):
        for side in range(2):
            dir_copy(half, side, step).wait_recv()
            dir_copy(half, side, step).wait_send()

        @pl.when(south)
        def _():
            row_copy(half, 0, step).wait_recv()
            row_copy(half, 1, step).wait_send()

        @pl.when(north)
        def _():
            row_copy(half, 1, step).wait_recv()
            row_copy(half, 0, step).wait_send()

    def first_state(half):
        start = half * HALF
        west = (start - LANES) % LON
        east = (start + HALF) % LON

        @pl.loop(0, OWN)
        def _(i):
            for to, source, length in ((0, west, LANES), (LANES, start, HALF), (LANES + HALF, east, LANES)):
                masked = spectrum[i, :, source : source + length] * ocean[:, start + to : start + to + length]
                state[half, 0, i + 1, :, to : to + length] = masked
                rows_out[half, 0, 0, i, :, to : to + length] = masked[ROWS - 1 :, :]
                rows_out[half, 0, 1, i, :, to : to + length] = masked[:1, :]

    first_state(0)
    pl.semaphore_wait(barrier, TILES - 1 + jnp.where(south, 1, 0) + jnp.where(north, 1, 0))

    def cur_copy(t):
        return pltpu.make_async_remote_copy(
            src_ref=cat,
            dst_ref=gathered.at[me],
            send_sem=cur_send,
            recv_sem=cur_recv,
            device_id={"comp": (me + t) % TILES},
            device_id_type=MESH,
        )

    def beside_copy(side):
        return pltpu.make_async_remote_copy(
            src_ref=cat,
            dst_ref=beside.at[side],
            send_sem=beside_send.at[side],
            recv_sem=beside_recv.at[side],
            device_id={"band": band + 1 - 2 * side},
            device_id_type=MESH,
        )

    start_edges(0, 0)

    @pl.loop(1, TILES)
    def _(t):
        cur_copy(t).start()

    pltpu.make_async_copy(cat, gathered.at[me], cur_recv).start()

    first_state(1)
    start_edges(1, 0)

    @pl.when(north)
    def _():
        beside_copy(0).start()

    @pl.when(south)
    def _():
        beside_copy(1).start()

    @pl.when(band == 0)
    def _():
        rows_in[:, :, 0] = jnp.zeros((2, SUBSTEPS, OWN, 1, REGION), f32)

    @pl.when(band == 3)
    def _():
        rows_in[:, :, 1] = jnp.zeros((2, SUBSTEPS, OWN, 1, REGION), f32)

    own_class = classes[rows8, :]
    turned = jnp.zeros((ROWS, LON), f32)
    for level in range(CLASSES):
        turned = jnp.where(own_class == level, refraction[level, freq], turned)
    store_wrapped(turning, turned)

    for offset in range(3):
        there = jnp.minimum(jnp.maximum(band + offset - 1, 0), 3)
        for col in range(LON // LANES):
            masks[offset, col] = sea[
                pl.ds(pl.multiple_of(there * ROWS, ROWS), ROWS), col * LANES : (col + 1) * LANES
            ].astype(f32)

    def store_split(part, rows, value):
        high = value.astype(bf16)
        split[part, rows, :] = high
        split[2 + part, rows, :] = (value - high.astype(f32)).astype(bf16)

    load_interp.wait()

    @pl.loop(0, COMPS // LANES)
    def _(b):
        span = pl.ds(pl.multiple_of(b * LANES, LANES), LANES)
        store_split(0, span, interp[span, :])
        store_split(1, span, interp[:, span].T)

    wait_bytes(gathered, cur_recv)

    lane = lax.broadcasted_iota(jnp.int32, (ROWS, LANES), 1)
    left = lane < 64
    for u in range(TILES // 2):
        one = gathered[inverse[2 * u]]
        two = gathered[inverse[2 * u + 1]]
        east_part = 0.025 * jnp.where(left, one, pltpu.roll(two, 64, 1))
        north_part = 0.025 * jnp.where(left, pltpu.roll(one, 64, 1), two)
        for place in (u + 1,) + ((0,) if u == TILES // 2 - 1 else ()) + ((TILES // 2 + 1,) if u == 0 else ()):
            at = slice(place * LANES, (place + 1) * LANES)
            base_u[:, at] = east_part
            base_v[:, at] = north_part

    row = lax.broadcasted_iota(jnp.int32, (ROWS, PIECE), 0)
    speed = courant[freq]

    def advanced(half, step, i, piece):
        lo = piece * PIECE
        at = slice(lo, lo + PIECE)
        fixed = slice(half * HALF + lo, half * HALF + lo + PIECE)
        centre = state[half, step, i + 1, :, at]
        west_lo = lo - LANES if lo else REGION - LANES
        east_lo = (lo + PIECE) % REGION
        west_piece = state[half, step, i + 1, :, west_lo : west_lo + LANES]
        east_piece = state[half, step, i + 1, :, east_lo : east_lo + LANES]
        wide = jnp.concatenate([west_piece, centre, east_piece], axis=1)
        west = pltpu.roll(wide, 1, 1)[:, LANES:-LANES]
        east = pltpu.roll(wide, PIECE + 2 * LANES - 1, 1)[:, LANES:-LANES]
        below = jnp.where(row == 0, rows_in[half, step, 0, i, :, at], pltpu.roll(centre, 1, 0))
        above = jnp.where(row == ROWS - 1, rows_in[half, step, 1, i, :, at], pltpu.roll(centre, ROWS - 1, 0))
        before = state[half, step, i, :, at]
        after = state[half, step, i + 2, :, at]
        cos_d = cosine[first_dir + i]
        ax = base_u[:, fixed] + speed * cos_d
        ay = base_v[:, fixed] + speed * sine[first_dir + i]
        turn = turning[:, fixed] * cos_d
        change = (
            jnp.maximum(ax, 0.0) * (centre - west) + jnp.minimum(ax, 0.0) * (east - centre)
            + (jnp.maximum(ay, 0.0) * (centre - below) + jnp.minimum(ay, 0.0) * (above - centre))
            + (jnp.maximum(turn, 0.0) * (centre - before) + jnp.minimum(turn, 0.0) * (after - centre))
        )
        return ocean[:, fixed] * (centre - change)

    def propagate(half):
        for step in range(SUBSTEPS - 1):
            finish_edges(half, step)

            @pl.loop(0, OWN)
            def _(i):
                for piece in range(REGION // PIECE):
                    at = slice(piece * PIECE, (piece + 1) * PIECE)
                    new = advanced(half, step, i, piece)
                    state[half, step + 1, i + 1, :, at] = new
                    rows_out[half, step + 1, 0, i, :, at] = new[ROWS - 1 :, :]
                    rows_out[half, step + 1, 1, i, :, at] = new[:1, :]

            start_edges(half, step + 1)

        finish_edges(half, SUBSTEPS - 1)

        @pl.loop(0, OWN)
        def _(i):
            for piece in range(REGION // PIECE):
                new = advanced(half, SUBSTEPS - 1, i, piece)
                for tile in range(PIECE // LANES):
                    place = piece * (PIECE // LANES) + tile
                    if 1 <= place <= HALF // LANES:
                        col = half * (HALF // LANES) + place - 1
                        first = (col // 4) * ROWS * BLOCK + col % 4
                        send1[pl.ds(first + i * 4, ROWS, stride=BLOCK), :] = new[:, tile * LANES : (tile + 1) * LANES]

        @pl.loop(0, TILES // 2)
        def _(k):
            spot = (low + k) % 4
            to = (
                ((plane + plane_offset(k // 4)) % PLANE) * PLANE + (spot // 2) * 4 + half * 2 + spot % 2
            )

            @pl.when(to != me)
            def _():
                pltpu.make_async_remote_copy(
                    src_ref=block_of(send1, order_of(to)),
                    dst_ref=block_of(recv1, me),
                    send_sem=in_send,
                    recv_sem=in_recv,
                    device_id={"comp": to},
                    device_id_type=MESH,
                ).start()

            @pl.when(to == me)
            def _():
                pltpu.make_async_copy(block_of(send1, order_of(to)), block_of(recv1, me), in_recv).start()

    propagate(0)
    propagate(1)
    wait_bytes(recv1, in_recv)

    @pl.loop(0, COMPS // CHUNK)
    def _(c):
        rows = pl.ds(pl.multiple_of(c * CHUNK, 16), CHUNK)
        for q in range(4):
            value = recv1[pl.ds(c * (CHUNK * 4) + q, CHUNK, stride=4), :]
            at = slice(q * LANES, (q + 1) * LANES)
            high = value.astype(bf16)
            points[rows, at] = value
            points_hi[rows, at] = high
            points_lo[rows, at] = (value - high.astype(f32)).astype(bf16)

    my_group = my_order // PLANE

    def source_chunk(c, drift):
        group = (plane + plane_offset(c)) % PLANE
        rows = pl.ds(pl.multiple_of(group * CHUNK, 16), CHUNK)
        matrix = jnp.concatenate([split[part, rows, :] for part in range(4)], axis=0)
        both = jnp.dot(matrix, points_hi[...], preferred_element_type=f32)
        more = jnp.dot(matrix[: 2 * CHUNK], points_lo[...], preferred_element_type=f32)
        sums = both[: 2 * CHUNK] + (both[2 * CHUNK :] + more)
        forward, backward = sums[:CHUNK], sums[CHUNK:]
        wave = points[rows, :]
        new = wave + 0.5 * (forward * backward - 0.5 * wave * (forward + backward))
        for q in range(4):
            send2[pl.ds(group * (CHUNK * 4) + q, CHUNK, stride=4), :] = new[:, q * LANES : (q + 1) * LANES]

        @pl.loop(0, PLANE)
        def _(e):
            to = group * PLANE + (low + e) % PLANE

            @pl.when(to != me)
            def _():
                pltpu.make_async_remote_copy(
                    src_ref=block_of(send2, to),
                    dst_ref=block_of(recv2, my_order),
                    send_sem=out_send,
                    recv_sem=out_recv.at[my_group],
                    device_id={"comp": to},
                    device_id_type=MESH,
                ).start()

            @pl.when(to == me)
            def _():
                pltpu.make_async_copy(
                    block_of(send2, me), block_of(recv2, my_order), out_recv.at[my_group]
                ).start()

        held = weights[rows, :]
        return tuple(
            drift[a] + jnp.sum((held[:, a : a + 1] * new).reshape(CHUNK // 8, 8, POINTS), axis=0) for a in range(2)
        )

    drift = lax.fori_loop(
        0, PLANE, source_chunk, (jnp.zeros((8, POINTS), f32), jnp.zeros((8, POINTS), f32))
    )
    for a in range(2):
        total = jnp.sum(drift[a], axis=0, keepdims=True)
        for q in range(4):
            drift_block[a * 4 + q : a * 4 + q + 1, :] = total[:, q * LANES : (q + 1) * LANES]

    my_drift = drift_all.at[my_order]

    @pl.loop(1, TILES)
    def _(t):
        pltpu.make_async_remote_copy(
            src_ref=drift_block,
            dst_ref=my_drift,
            send_sem=drift_send,
            recv_sem=drift_recv,
            device_id={"comp": (me + t) % TILES},
            device_id_type=MESH,
        ).start()

    pltpu.make_async_copy(drift_block, my_drift, drift_recv).start()

    wait_bytes(gathered.at[: TILES - 1], cur_send)
    wait_bytes(recv1.at[: (TILES - 1) * BLOCK], in_send)

    @pl.when(north)
    def _():
        beside_copy(0).wait_send()
        beside_copy(1).wait_recv()

    @pl.when(south)
    def _():
        beside_copy(1).wait_send()
        beside_copy(0).wait_recv()

    @pl.loop(0, PLANE)
    def _(g):
        group_rows = pl.ds(pl.multiple_of(g * PLANE * BLOCK, 8), PLANE * BLOCK)
        wait_bytes(recv2.at[group_rows], out_recv.at[g])

        @pl.loop(0, OWN)
        def _(i):
            for q in range(4):
                cols = pl.ds(pl.multiple_of(g * 4 * LANES + q * LANES, LANES), LANES)
                out[i, :, cols] = recv2[pl.ds(g * PLANE * BLOCK + q + i * 4, ROWS, stride=BLOCK), :]

        cols = pl.ds(pl.multiple_of(g * 4 * LANES, LANES), 4 * LANES)
        pltpu.make_async_copy(out.at[:, :, cols], out_any.at[:, :, cols], store_sem).start()

    wait_bytes(drift_all, drift_recv)
    tile = owner[me]
    row1 = lax.broadcasted_iota(jnp.int32, (ROWS, LANES), 0)

    def twice(value, half):
        other = pltpu.roll(value, 64, 1)
        return jnp.where(half == 0, value, other), jnp.where(half == 0, other, value)

    def mask(which_tile, offset):
        at_left, at_right = twice(masks[offset + 1, which_tile // 2], which_tile % 2)
        return jnp.where(left, at_left, at_right)

    own = mask(tile, 0)
    held = cat[...] * own
    west_tile, east_tile = (tile + TILES - 1) % TILES, (tile + 1) % TILES
    held_w = gathered[inverse[west_tile]] * mask(west_tile, 0)
    held_e = gathered[inverse[east_tile]] * mask(east_tile, 0)
    held_s = jnp.where(south, beside[0] * mask(tile, -1), 0.0)
    held_n = jnp.where(north, beside[1] * mask(tile, 1), 0.0)
    west = jnp.where(lane % 64 == 0, pltpu.roll(held_w, 65, 1), pltpu.roll(held, 1, 1))
    east = jnp.where(lane % 64 == 63, pltpu.roll(held_e, 63, 1), pltpu.roll(held, 127, 1))
    below = jnp.where(row1 == 0, pltpu.roll(held_s, 1, 0), pltpu.roll(held, 1, 0))
    above = jnp.where(row1 == ROWS - 1, pltpu.roll(held_n, 7, 0), pltpu.roll(held, 7, 0))
    lap = west + east + below + above - 4.0 * held
    quarter = (tile % 8) // 2
    sums = [jnp.zeros((ROWS, LANES), f32), jnp.zeros((ROWS, LANES), f32)]
    for r in range(ROWS):
        piece = drift_all[(tile // 8) * ROWS + r]
        for a in range(2):
            chosen = jnp.sum(jnp.where(row1 == quarter + 4 * a, piece, 0.0), axis=0, keepdims=True)
            sums[a] = jnp.where(row1 == r, chosen, sums[a])
    eastward, _ = twice(sums[0], tile % 2)
    _, northward = twice(sums[1], tile % 2)
    stokes = jnp.where(left, eastward, northward)
    turn = jnp.where(left, 1.0, -1.0) * coriolis[rows8, :]
    other = pltpu.roll(held + stokes, 64, 1)
    result = own * (held + 0.5 * (turn * other + 0.2 * lap - 0.1 * held))
    ocean_out[0] = result[:, :64]
    ocean_out[1] = result[:, 64:]

    wait_bytes(drift_all.at[: TILES - 1], drift_send)
    wait_bytes(recv2.at[: (TILES - 1) * BLOCK], out_send)
    wait_bytes(out, store_sem)


def tables():
    angles = np.arange(DIRS, dtype=np.float32) * np.float32(2.0 * math.pi / DIRS)
    cosine, sine = np.cos(angles).astype(np.float32), np.sin(angles).astype(np.float32)
    k = np.arange(COMPS)
    scale = (np.float32(0.2) * (k // DIRS + 1).astype(np.float32) / np.float32(FREQ)).astype(np.float32)
    weights = np.stack([scale * cosine[k % DIRS], scale * sine[k % DIRS]], axis=1)
    latitude = -1.2 + 2.4 * (np.arange(TOTAL_ROWS, dtype=np.float32) + np.float32(0.5)) / TOTAL_ROWS
    coriolis = np.broadcast_to(np.sin(latitude.astype(np.float32))[:, None], (TOTAL_ROWS, LANES))
    return cosine, sine, weights.astype(np.float32), coriolis.astype(np.float32)


def local(spectrum, currents, group_courant, refraction, interp, sea_mask, depth_class, owner_map):
    cosine, sine, weights, coriolis = tables()
    index = jnp.arange(TILES, dtype=jnp.int32)
    inverse = jnp.sum(jnp.where(owner_map[None, :] == index[:, None], index[None, :], 0), axis=1)
    vmem, smem = pl.BlockSpec(memory_space=pltpu.VMEM), pl.BlockSpec(memory_space=pltpu.SMEM)
    anywhere = pl.BlockSpec(memory_space=pl.ANY)
    dma = pltpu.SemaphoreType.DMA
    extended = pltpu.VMEM((ROWS, LON + 2 * LANES), f32)
    blocks = pltpu.VMEM((TILES * BLOCK, LANES), f32)
    edge_rows = pltpu.VMEM((2, SUBSTEPS, 2, OWN, 1, REGION), f32)
    return pl.pallas_call(
        wave_kernel,
        out_shape=(
            jax.ShapeDtypeStruct((OWN, ROWS, LON), f32),
            jax.ShapeDtypeStruct((2, ROWS, LON // TILES), f32),
        ),
        in_specs=[vmem, vmem, vmem, vmem, anywhere, vmem, vmem] + [smem] * 6,
        out_specs=(anywhere, vmem),
        scratch_shapes=[
            pltpu.VMEM((2, SUBSTEPS, OWN + 2, ROWS, REGION), f32),
            edge_rows,
            edge_rows,
            extended,
            extended,
            extended,
            extended,
            blocks,
            blocks,
            blocks,
            blocks,
            pltpu.VMEM((OWN, ROWS, LON), f32),
            pltpu.VMEM((COMPS, COMPS), f32),
            pltpu.VMEM((4, COMPS, COMPS), bf16),
            pltpu.VMEM((COMPS, POINTS), f32),
            pltpu.VMEM((COMPS, POINTS), bf16),
            pltpu.VMEM((COMPS, POINTS), bf16),
            pltpu.VMEM((ROWS, LANES), f32),
            pltpu.VMEM((TILES, ROWS, LANES), f32),
            pltpu.VMEM((2, ROWS, LANES), f32),
            pltpu.VMEM((8, LANES), f32),
            pltpu.VMEM((TILES, 8, LANES), f32),
            pltpu.VMEM((3, LON // LANES, ROWS, LANES), f32),
            dma,
            dma,
            dma,
            dma((2,)),
            dma((2,)),
            dma((2, SUBSTEPS, 4)),
            dma((2, SUBSTEPS, 4)),
            dma,
            dma,
            dma,
            dma((PLANE,)),
            dma,
            dma,
            dma,
        ],
        compiler_params=pltpu.CompilerParams(
            collective_id=0, has_side_effects=True, vmem_limit_bytes=62 * 2**20
        ),
        name="waves",
    )(
        spectrum, currents, sea_mask, depth_class, interp, jnp.asarray(weights), jnp.asarray(coriolis), group_courant,
        refraction, owner_map, inverse, jnp.asarray(cosine), jnp.asarray(sine),
    )


def solution(mesh):
    in_specs = (P("comp", "band", None), P(None, "band", "comp"), P(), P(), P(), P(), P(), P())
    out_specs = (P("comp", "band", None), P(None, "band", "comp"))
    return jax.shard_map(local, mesh=mesh, in_specs=in_specs, out_specs=out_specs, check_vma=False)
```

time: 202 us -> 189 us (0.936)
  Pallas kernels: 193 us -> 183 us
    pallas_call x2 -> x1, Pallas kernels: 193 us -> 183 us  [local(): pl.pallas_call(wave_kernel, out_shape=(jax.ShapeDtypeStruct((OWN, ROWS, L...]
    unnamed x18 -> x4, local copies, waits for them, and re-layouts: 4.27 us -> 3.88 us
where the time goes in v2:
time: 189 us
  Pallas kernels  183 us (97%)
  local copies, waits for them, and re-layouts  3.88 us (2%)
    pallas_call x1, Pallas kernels, local(): pl.pallas_call(wave_kernel, out_shape=(jax.ShapeDtypeStruct((OWN, ROWS, L...  183 us
    unnamed x4, local copies, waits for them, and re-layouts  3.88 us

profile of v2, /device:TPU:1, one launch (start us, length us, event | category | flops | bytes accessed | tf_op | source)
XLA Modules:
  0.0 188.6 jit_solution(1525900076397677486)
XLA Ops:
  0.6 1.3 select_reduce_fusion.inverse
  1.9 182.8 %waves.1 = (f32[18,8,4096]{2,1,0:T(8,128)}, f32[2,8,64]{2,1,0:T(8,128)}) custom-call(f32[18,8,4096]{2,1,0:T(8,128)} %spectrum.1, f32[2,8,64]{2,1,0:T(8,128)} %currents.1, s32[32,4096]{1,0:T(8,128)} %sea.1, s32[32,4096]{1,0:T(8,128)} %classes.1, f32[1152,1152]{1,0:T(8,128)} %interp_any.1, f32[1152,2]{1,0:T(8,128)} %constant.10.clone.weights, ...), custom_call_target="tpu_custom_call" | custom-call | tf_op jit(solution)/shard_map/waves/pallas_call | solution.py:499
  184.7 0.0 copy-start
  184.7 3.3 %copy.16 = f32[18,8,4096]{2,1,0:T(8,128)} copy(f32[18,8,4096]{2,1,0:T(8,128)} %get-tuple-element.4) | data formatting | bytes 4718592
  188.0 0.0 copy-done
  188.0 0.6 copy.17
Async XLA Ops:
  184.7 3.3 %copy-start = (f32[2,8,64]{2,1,0:T(8,128)S(1)}, f32[2,8,64]{2,1,0:T(8,128)}, u32[]{:S(2)}) copy-start(f32[2,8,64]{2,1,0:T(8,128)} %get-tuple-element.5) | copy-start | bytes 12292

commit v3 on v2

--- a/solution.py
+++ b/solution.py
@@ -23,9 +23,12 @@
 BLOCK = OWN * 4
 CHUNK = 144
 POINTS = 512
+PIECE = 1024
 HALF = 2048
-REGION = HALF + 2 * LANES
-PIECE = 1152
+HALO = 4
+WIDE = OWN + 2 * HALO
+PAIRS = ((4, 0), (3, 7), (5, 1), (2, 6))
+INNER = (4, 14)
 MESH = pl.DeviceIdType.MESH
 f32 = jnp.float32
 bf16 = jnp.bfloat16
@@ -35,10 +38,6 @@
     return 4 + (1 - 2 * (step % 2)) * ((step + 1) // 2)
 
 
-def order_of(device):
-    return (device // 2) % 2 * (TILES // 2) + device // 4 * 2 + device % 2
-
-
 def block_of(ref, which):
     return ref.at[pl.ds(pl.multiple_of(which * BLOCK, 8), BLOCK)]
 
@@ -48,11 +47,11 @@
 
 
 def wave_kernel(
-    spectrum, currents, sea, classes, interp_any, weights, coriolis, courant, refraction, owner, inverse, cosine, sine,
+    spectrum_any, currents, sea, classes, interp_any, weights, coriolis, courant, refraction, owner, inverse, cosine, sine,
     out_any, ocean_out,
     state, rows_out, rows_in, base_u, base_v, turning, ocean, send1, recv1, send2, recv2, out, interp, split,
     points, points_hi, points_lo, cat, gathered, beside, drift_block, drift_all, masks,
-    interp_sem, cur_send, cur_recv, beside_send, beside_recv, edge_send, edge_recv,
+    interp_sem, spec_sem, cur_send, cur_recv, beside_send, beside_recv, row_send, row_recv, dir_send, dir_recv,
     in_send, in_recv, out_send, out_recv, drift_send, drift_recv, store_sem,
 ):
     me = lax.axis_index("comp")
@@ -62,12 +61,13 @@
     partner = me + 1 - 2 * (me % 2)
     freq = me // 2
     first_dir = (me % 2) * OWN
-    my_order = order_of(me)
     south = band > 0
     north = band < 3
 
     load_interp = pltpu.make_async_copy(interp_any, interp, interp_sem)
     load_interp.start()
+    load_spectrum = pltpu.make_async_copy(spectrum_any, state.at[0, HALO : HALO + OWN], spec_sem)
+    load_spectrum.start()
 
     barrier = pltpu.get_barrier_semaphore()
 
@@ -85,76 +85,82 @@
 
     rows8 = pl.ds(pl.multiple_of(band * ROWS, ROWS), ROWS)
 
-    def store_wrapped(ref, value):
-        ref[:, LANES : LANES + LON] = value
-        ref[:, :LANES] = value[:, LON - LANES :]
-        ref[:, LANES + LON :] = value[:, :LANES]
-
-    store_wrapped(ocean, sea[rows8, :].astype(f32))
+    ocean[...] = sea[rows8, :].astype(f32)
     cat[:, :64] = currents[0]
     cat[:, 64:] = currents[1]
 
-    def row_copy(half, side, step):
+    def span(step, part):
+        return ((5 + step, 21 - step), (1 + step, 5 + step), (21 - step, 25 - step))[part]
+
+    def row_copy(step, part, half, side):
+        lo, hi = span(step, part)
+        cols = slice(half * HALF, (half + 1) * HALF)
         return pltpu.make_async_remote_copy(
-            src_ref=rows_out.at[half, step, side],
-            dst_ref=rows_in.at[half, step, side],
-            send_sem=edge_send.at[half, step, side],
-            recv_sem=edge_recv.at[half, step, side],
+            src_ref=rows_out.at[step, side, lo:hi, :, cols],
+            dst_ref=rows_in.at[step, side, lo:hi, :, cols],
+            send_sem=row_send.at[step, part, half, side],
+            recv_sem=row_recv.at[step, part, half, side],
             device_id={"band": band + 1 - 2 * side},
             device_id_type=MESH,
         )
 
-    def dir_copy(half, side, step):
+    def start_rows(step, parts, halves=(0, 1)):
+        @pl.when(north)
+        def _():
+            for part in parts:
+                for half in halves:
+                    row_copy(step, part, half, 0).start()
+
+        @pl.when(south)
+        def _():
+            for part in parts:
+                for half in halves:
+                    row_copy(step, part, half, 1).start()
+
+    def finish_rows(step, parts, halves=(0, 1)):
+        @pl.when(south)
+        def _():
+            for part in parts:
+                for half in halves:
+                    row_copy(step, part, half, 0).wait_recv()
+                    row_copy(step, part, half, 1).wait_send()
+
+        @pl.when(north)
+        def _():
+            for part in parts:
+                for half in halves:
+                    row_copy(step, part, half, 1).wait_recv()
+                    row_copy(step, part, half, 0).wait_send()
+
+    pieces = ((0, 2), (2, 3), (3, 4))
+
+    def dir_copy(side, n):
+        lo, hi = pieces[n]
+        source = (OWN - HALO if side == 0 else 0) + lo
+        to = (0 if side == 0 else HALO + OWN) + lo
         return pltpu.make_async_remote_copy(
-            src_ref=state.at[half, step, OWN if side == 0 else 1],
-            dst_ref=state.at[half, step, 0 if side == 0 else OWN + 1],
-            send_sem=edge_send.at[half, step, 2 + side],
-            recv_sem=edge_recv.at[half, step, 2 + side],
+            src_ref=spectrum_any.at[source : source + hi - lo],
+            dst_ref=state.at[0, to : to + hi - lo],
+            send_sem=dir_send.at[side, n],
+            recv_sem=dir_recv.at[side, n],
             device_id={"comp": partner},
             device_id_type=MESH,
         )
 
-    def start_edges(half, step):
-        @pl.when(north)
-        def _():
-            row_copy(half, 0, step).start()
-
-        @pl.when(south)
-        def _():
-            row_copy(half, 1, step).start()
-
-        dir_copy(half, 0, step).start()
-        dir_copy(half, 1, step).start()
-
-    def finish_edges(half, step):
-        for side in range(2):
-            dir_copy(half, side, step).wait_recv()
-            dir_copy(half, side, step).wait_send()
-
-        @pl.when(south)
-        def _():
-            row_copy(half, 0, step).wait_recv()
-            row_copy(half, 1, step).wait_send()
-
-        @pl.when(north)
-        def _():
-            row_copy(half, 1, step).wait_recv()
-            row_copy(half, 0, step).wait_send()
-
-    def first_state(half):
-        start = half * HALF
-        west = (start - LANES) % LON
-        east = (start + HALF) % LON
-
-        @pl.loop(0, OWN)
-        def _(i):
-            for to, source, length in ((0, west, LANES), (LANES, start, HALF), (LANES + HALF, east, LANES)):
-                masked = spectrum[i, :, source : source + length] * ocean[:, start + to : start + to + length]
-                state[half, 0, i + 1, :, to : to + length] = masked
-                rows_out[half, 0, 0, i, :, to : to + length] = masked[ROWS - 1 :, :]
-                rows_out[half, 0, 1, i, :, to : to + length] = masked[:1, :]
-
-    first_state(0)
+    def start_dirs(n):
+        dir_copy(0, n).start()
+        dir_copy(1, n).start()
+
+    def mask_first(lo, hi):
+        @pl.loop(lo, hi)
+        def _(e):
+            masked = state[0, e] * ocean[...]
+            state[0, e] = masked
+            rows_out[0, 0, e] = masked[ROWS - 1 :, :]
+            rows_out[0, 1, e] = masked[:1, :]
+
+    load_spectrum.wait()
+    mask_first(HALO, HALO + OWN)
     pl.semaphore_wait(barrier, TILES - 1 + jnp.where(south, 1, 0) + jnp.where(north, 1, 0))
 
     def cur_copy(t):
@@ -177,7 +183,7 @@
             device_id_type=MESH,
         )
 
-    start_edges(0, 0)
+    start_rows(0, (0,))
 
     @pl.loop(1, TILES)
     def _(t):
@@ -185,8 +191,7 @@
 
     pltpu.make_async_copy(cat, gathered.at[me], cur_recv).start()
 
-    first_state(1)
-    start_edges(1, 0)
+    start_dirs(0)
 
     @pl.when(north)
     def _():
@@ -198,17 +203,17 @@
 
     @pl.when(band == 0)
     def _():
-        rows_in[:, :, 0] = jnp.zeros((2, SUBSTEPS, OWN, 1, REGION), f32)
+        rows_in[:, 0] = jnp.zeros((SUBSTEPS, WIDE, 1, LON), f32)
 
     @pl.when(band == 3)
     def _():
-        rows_in[:, :, 1] = jnp.zeros((2, SUBSTEPS, OWN, 1, REGION), f32)
+        rows_in[:, 1] = jnp.zeros((SUBSTEPS, WIDE, 1, LON), f32)
 
     own_class = classes[rows8, :]
     turned = jnp.zeros((ROWS, LON), f32)
     for level in range(CLASSES):
         turned = jnp.where(own_class == level, refraction[level, freq], turned)
-    store_wrapped(turning, turned)
+    turning[...] = turned
 
     for offset in range(3):
         there = jnp.minimum(jnp.maximum(band + offset - 1, 0), 3)
@@ -239,81 +244,78 @@
         two = gathered[inverse[2 * u + 1]]
         east_part = 0.025 * jnp.where(left, one, pltpu.roll(two, 64, 1))
         north_part = 0.025 * jnp.where(left, pltpu.roll(one, 64, 1), two)
-        for place in (u + 1,) + ((0,) if u == TILES // 2 - 1 else ()) + ((TILES // 2 + 1,) if u == 0 else ()):
-            at = slice(place * LANES, (place + 1) * LANES)
-            base_u[:, at] = east_part
-            base_v[:, at] = north_part
+        at = slice(u * LANES, (u + 1) * LANES)
+        base_u[:, at] = east_part
+        base_v[:, at] = north_part
 
     row = lax.broadcasted_iota(jnp.int32, (ROWS, PIECE), 0)
     speed = courant[freq]
 
-    def advanced(half, step, i, piece):
+    def advanced(step, e, piece):
         lo = piece * PIECE
         at = slice(lo, lo + PIECE)
-        fixed = slice(half * HALF + lo, half * HALF + lo + PIECE)
-        centre = state[half, step, i + 1, :, at]
-        west_lo = lo - LANES if lo else REGION - LANES
-        east_lo = (lo + PIECE) % REGION
-        west_piece = state[half, step, i + 1, :, west_lo : west_lo + LANES]
-        east_piece = state[half, step, i + 1, :, east_lo : east_lo + LANES]
+        centre = state[step, e, :, at]
+        west_lo, east_lo = (lo - LANES) % LON, (lo + PIECE) % LON
+        west_piece = state[step, e, :, west_lo : west_lo + LANES]
+        east_piece = state[step, e, :, east_lo : east_lo + LANES]
         wide = jnp.concatenate([west_piece, centre, east_piece], axis=1)
         west = pltpu.roll(wide, 1, 1)[:, LANES:-LANES]
         east = pltpu.roll(wide, PIECE + 2 * LANES - 1, 1)[:, LANES:-LANES]
-        below = jnp.where(row == 0, rows_in[half, step, 0, i, :, at], pltpu.roll(centre, 1, 0))
-        above = jnp.where(row == ROWS - 1, rows_in[half, step, 1, i, :, at], pltpu.roll(centre, ROWS - 1, 0))
-        before = state[half, step, i, :, at]
-        after = state[half, step, i + 2, :, at]
-        cos_d = cosine[first_dir + i]
-        ax = base_u[:, fixed] + speed * cos_d
-        ay = base_v[:, fixed] + speed * sine[first_dir + i]
-        turn = turning[:, fixed] * cos_d
+        below = jnp.where(row == 0, rows_in[step, 0, e, :, at], pltpu.roll(centre, 1, 0))
+        above = jnp.where(row == ROWS - 1, rows_in[step, 1, e, :, at], pltpu.roll(centre, ROWS - 1, 0))
+        before = state[step, e - 1, :, at]
+        after = state[step, e + 1, :, at]
+        direction = (first_dir + e + DIRS - HALO) % DIRS
+        cos_d = cosine[direction]
+        ax = base_u[:, at] + speed * cos_d
+        ay = base_v[:, at] + speed * sine[direction]
+        turn = turning[:, at] * cos_d
         change = (
             jnp.maximum(ax, 0.0) * (centre - west) + jnp.minimum(ax, 0.0) * (east - centre)
             + (jnp.maximum(ay, 0.0) * (centre - below) + jnp.minimum(ay, 0.0) * (above - centre))
             + (jnp.maximum(turn, 0.0) * (centre - before) + jnp.minimum(turn, 0.0) * (after - centre))
         )
-        return ocean[:, fixed] * (centre - change)
-
-    def propagate(half):
-        for step in range(SUBSTEPS - 1):
-            finish_edges(half, step)
-
-            @pl.loop(0, OWN)
-            def _(i):
-                for piece in range(REGION // PIECE):
-                    at = slice(piece * PIECE, (piece + 1) * PIECE)
-                    new = advanced(half, step, i, piece)
-                    state[half, step + 1, i + 1, :, at] = new
-                    rows_out[half, step + 1, 0, i, :, at] = new[ROWS - 1 :, :]
-                    rows_out[half, step + 1, 1, i, :, at] = new[:1, :]
-
-            start_edges(half, step + 1)
-
-        finish_edges(half, SUBSTEPS - 1)
-
-        @pl.loop(0, OWN)
-        def _(i):
-            for piece in range(REGION // PIECE):
-                new = advanced(half, SUBSTEPS - 1, i, piece)
+        return ocean[:, at] * (centre - change)
+
+    def middle(step, part, halves=(0, 1)):
+        lo, hi = span(step, part)
+
+        @pl.loop(lo, hi)
+        def _(e):
+            for piece in range(halves[0] * 2, halves[-1] * 2 + 2):
+                at = slice(piece * PIECE, (piece + 1) * PIECE)
+                new = advanced(step, e, piece)
+                state[step + 1, e, :, at] = new
+                rows_out[step + 1, 0, e, :, at] = new[ROWS - 1 :, :]
+                rows_out[step + 1, 1, e, :, at] = new[:1, :]
+
+    def last(part, halves=(0, 1)):
+        lo, hi = span(SUBSTEPS - 1, part)
+
+        @pl.loop(lo, hi)
+        def _(e):
+            for piece in range(halves[0] * 2, halves[-1] * 2 + 2):
+                new = advanced(SUBSTEPS - 1, e, piece)
                 for tile in range(PIECE // LANES):
-                    place = piece * (PIECE // LANES) + tile
-                    if 1 <= place <= HALF // LANES:
-                        col = half * (HALF // LANES) + place - 1
-                        first = (col // 4) * ROWS * BLOCK + col % 4
-                        send1[pl.ds(first + i * 4, ROWS, stride=BLOCK), :] = new[:, tile * LANES : (tile + 1) * LANES]
-
-        @pl.loop(0, TILES // 2)
+                    col = piece * (PIECE // LANES) + tile
+                    first = (col // 4) * ROWS * BLOCK + col % 4
+                    send1[pl.ds(first + (e - HALO) * 4, ROWS, stride=BLOCK), :] = (
+                        new[:, tile * LANES : (tile + 1) * LANES]
+                    )
+
+    def send_blocks(group, lo, hi):
+        @pl.loop(0, 16)
         def _(k):
-            spot = (low + k) % 4
-            to = (
-                ((plane + plane_offset(k // 4)) % PLANE) * PLANE + (spot // 2) * 4 + half * 2 + spot % 2
-            )
+            away = jnp.where(k < 8, PAIRS[group][0], PAIRS[group][1])
+            to = ((plane + away) % PLANE) * PLANE + (low + k) % PLANE
+            source = send1.at[pl.ds(pl.multiple_of(to * BLOCK + lo * 4, 8), (hi - lo) * 4)]
+            target = recv1.at[pl.ds(pl.multiple_of(me * BLOCK + lo * 4, 8), (hi - lo) * 4)]
 
             @pl.when(to != me)
             def _():
                 pltpu.make_async_remote_copy(
-                    src_ref=block_of(send1, order_of(to)),
-                    dst_ref=block_of(recv1, me),
+                    src_ref=source,
+                    dst_ref=target,
                     send_sem=in_send,
                     recv_sem=in_recv,
                     device_id={"comp": to},
@@ -322,10 +324,38 @@
 
             @pl.when(to == me)
             def _():
-                pltpu.make_async_copy(block_of(send1, order_of(to)), block_of(recv1, me), in_recv).start()
-
-    propagate(0)
-    propagate(1)
+                pltpu.make_async_copy(source, target, in_recv).start()
+
+    inner, sides = (0,), (1, 2)
+    for step in range(SUBSTEPS - 1):
+        for half in range(2):
+            finish_rows(step, inner, (half,))
+            middle(step, 0, (half,))
+            start_rows(step + 1, inner, (half,))
+        if step < 2:
+            start_dirs(step + 1)
+    for half in range(2):
+        finish_rows(SUBSTEPS - 1, inner, (half,))
+        last(0, (half,))
+    for side in range(2):
+        for n in range(3):
+            dir_copy(side, n).wait()
+    mask_first(0, HALO)
+    mask_first(HALO + OWN, WIDE)
+    start_rows(0, sides)
+    send_blocks(0, *INNER)
+    for step in range(SUBSTEPS - 1):
+        finish_rows(step, sides)
+        middle(step, 1)
+        middle(step, 2)
+        start_rows(step + 1, sides)
+        send_blocks(step + 1, *INNER)
+    finish_rows(SUBSTEPS - 1, sides)
+    last(1)
+    last(2)
+    for group in range(4):
+        send_blocks(group, 0, HALO)
+        send_blocks(group, OWN - HALO, OWN)
     wait_bytes(recv1, in_recv)
 
     @pl.loop(0, COMPS // CHUNK)
@@ -339,7 +369,7 @@
             points_hi[rows, at] = high
             points_lo[rows, at] = (value - high.astype(f32)).astype(bf16)
 
-    my_group = my_order // PLANE
+    my_group = me // PLANE
 
     def source_chunk(c, drift):
         group = (plane + plane_offset(c)) % PLANE
@@ -362,7 +392,7 @@
             def _():
                 pltpu.make_async_remote_copy(
                     src_ref=block_of(send2, to),
-                    dst_ref=block_of(recv2, my_order),
+                    dst_ref=block_of(recv2, me),
                     send_sem=out_send,
                     recv_sem=out_recv.at[my_group],
                     device_id={"comp": to},
@@ -372,7 +402,7 @@
             @pl.when(to == me)
             def _():
                 pltpu.make_async_copy(
-                    block_of(send2, me), block_of(recv2, my_order), out_recv.at[my_group]
+                    block_of(send2, me), block_of(recv2, me), out_recv.at[my_group]
                 ).start()
 
         held = weights[rows, :]
@@ -388,7 +418,7 @@
         for q in range(4):
             drift_block[a * 4 + q : a * 4 + q + 1, :] = total[:, q * LANES : (q + 1) * LANES]
 
-    my_drift = drift_all.at[my_order]
+    my_drift = drift_all.at[me]
 
     @pl.loop(1, TILES)
     def _(t):
@@ -417,7 +447,8 @@
         beside_copy(0).wait_recv()
 
     @pl.loop(0, PLANE)
-    def _(g):
+    def _(n):
+        g = (plane + PLANE - plane_offset(n)) % PLANE
         group_rows = pl.ds(pl.multiple_of(g * PLANE * BLOCK, 8), PLANE * BLOCK)
         wait_bytes(recv2.at[group_rows], out_recv.at[g])
 
@@ -493,25 +524,25 @@
     vmem, smem = pl.BlockSpec(memory_space=pltpu.VMEM), pl.BlockSpec(memory_space=pltpu.SMEM)
     anywhere = pl.BlockSpec(memory_space=pl.ANY)
     dma = pltpu.SemaphoreType.DMA
-    extended = pltpu.VMEM((ROWS, LON + 2 * LANES), f32)
+    field = pltpu.VMEM((ROWS, LON), f32)
     blocks = pltpu.VMEM((TILES * BLOCK, LANES), f32)
-    edge_rows = pltpu.VMEM((2, SUBSTEPS, 2, OWN, 1, REGION), f32)
+    edge_rows = pltpu.VMEM((SUBSTEPS, 2, WIDE, 1, LON), f32)
     return pl.pallas_call(
         wave_kernel,
         out_shape=(
             jax.ShapeDtypeStruct((OWN, ROWS, LON), f32),
             jax.ShapeDtypeStruct((2, ROWS, LON // TILES), f32),
         ),
-        in_specs=[vmem, vmem, vmem, vmem, anywhere, vmem, vmem] + [smem] * 6,
+        in_specs=[anywhere, vmem, vmem, vmem, anywhere, vmem, vmem] + [smem] * 6,
         out_specs=(anywhere, vmem),
         scratch_shapes=[
-            pltpu.VMEM((2, SUBSTEPS, OWN + 2, ROWS, REGION), f32),
+            pltpu.VMEM((SUBSTEPS, WIDE, ROWS, LON), f32),
             edge_rows,
             edge_rows,
-            extended,
-            extended,
-            extended,
-            extended,
+            field,
+            field,
+            field,
+            field,
             blocks,
             blocks,
             blocks,
@@ -531,10 +562,13 @@
             dma,
             dma,
             dma,
+            dma,
             dma((2,)),
             dma((2,)),
-            dma((2, SUBSTEPS, 4)),
-            dma((2, SUBSTEPS, 4)),
+            dma((SUBSTEPS, 3, 2, 2)),
+            dma((SUBSTEPS, 3, 2, 2)),
+            dma((2, 3)),
+            dma((2, 3)),
             dma,
             dma,
             dma,

time: 189 us -> 180 us (0.952)
  Pallas kernels: 183 us -> 174 us
    pallas_call x1, Pallas kernels: 183 us -> 174 us  [local(): pl.pallas_call(wave_kernel, out_shape=(jax.ShapeDtypeStruct((OWN, ROWS, L...]
where the time goes in v3:
time: 180 us
  Pallas kernels  174 us (97%)
  local copies, waits for them, and re-layouts  3.88 us (2%)
    pallas_call x1, Pallas kernels, local(): pl.pallas_call(wave_kernel, out_shape=(jax.ShapeDtypeStruct((OWN, ROWS, L...  174 us
    unnamed x4, local copies, waits for them, and re-layouts  3.88 us

profile of v3, /device:TPU:1, one launch (start us, length us, event | category | flops | bytes accessed | tf_op | source)
XLA Modules:
  0.0 180.2 jit_solution(15370592798900760498)
XLA Ops:
  0.6 1.3 select_reduce_fusion.inverse
  1.9 174.4 %waves.1 = (f32[18,8,4096]{2,1,0:T(8,128)}, f32[2,8,64]{2,1,0:T(8,128)}) custom-call(f32[18,8,4096]{2,1,0:T(8,128)} %spectrum_any.1, f32[2,8,64]{2,1,0:T(8,128)} %currents.1, s32[32,4096]{1,0:T(8,128)} %sea.1, s32[32,4096]{1,0:T(8,128)} %classes.1, f32[1152,1152]{1,0:T(8,128)} %interp_any.1, f32[1152,2]{1,0:T(8,128)} %constant.10.clone.weights, ...), custom_call_target="tpu_custom_call" | custom-call | tf_op jit(solution)/shard_map/waves/pallas_call | solution.py:530
  176.3 0.0 copy-start
  176.3 3.3 %copy.16 = f32[18,8,4096]{2,1,0:T(8,128)} copy(f32[18,8,4096]{2,1,0:T(8,128)} %get-tuple-element.4) | data formatting | bytes 4718592
  179.6 0.0 copy-done
  179.6 0.6 copy.17
Async XLA Ops:
  176.3 3.3 %copy-start = (f32[2,8,64]{2,1,0:T(8,128)S(1)}, f32[2,8,64]{2,1,0:T(8,128)}, u32[]{:S(2)}) copy-start(f32[2,8,64]{2,1,0:T(8,128)} %get-tuple-element.5) | copy-start | bytes 12292

commit v4 on v3

--- a/solution.py
+++ b/solution.py
@@ -35,7 +35,7 @@
 
 
 def plane_offset(step):
-    return 4 + (1 - 2 * (step % 2)) * ((step + 1) // 2)
+    return 3 * (step + 1) % PLANE
 
 
 def block_of(ref, which):
@@ -64,10 +64,8 @@
     south = band > 0
     north = band < 3
 
-    load_interp = pltpu.make_async_copy(interp_any, interp, interp_sem)
-    load_interp.start()
-    load_spectrum = pltpu.make_async_copy(spectrum_any, state.at[0, HALO : HALO + OWN], spec_sem)
-    load_spectrum.start()
+    for n in range(0, OWN, 3):
+        pltpu.make_async_copy(spectrum_any.at[n : n + 3], state.at[0, HALO + n : HALO + n + 3], spec_sem).start()
 
     barrier = pltpu.get_barrier_semaphore()
 
@@ -78,10 +76,12 @@
     @pl.when(south)
     def _():
         pl.semaphore_signal(barrier, inc=1, device_id={"band": band - 1}, device_id_type=MESH)
+        pl.semaphore_signal(barrier, inc=1, device_id={"comp": partner, "band": band - 1}, device_id_type=MESH)
 
     @pl.when(north)
     def _():
         pl.semaphore_signal(barrier, inc=1, device_id={"band": band + 1}, device_id_type=MESH)
+        pl.semaphore_signal(barrier, inc=1, device_id={"comp": partner, "band": band + 1}, device_id_type=MESH)
 
     rows8 = pl.ds(pl.multiple_of(band * ROWS, ROWS), ROWS)
 
@@ -93,7 +93,7 @@
         return ((5 + step, 21 - step), (1 + step, 5 + step), (21 - step, 25 - step))[part]
 
     def row_copy(step, part, half, side):
-        lo, hi = span(step, part)
+        lo, hi = span(step, part) if step else (HALO, HALO + OWN)
         cols = slice(half * HALF, (half + 1) * HALF)
         return pltpu.make_async_remote_copy(
             src_ref=rows_out.at[step, side, lo:hi, :, cols],
@@ -131,6 +131,17 @@
                 for half in halves:
                     row_copy(step, part, half, 1).wait_recv()
                     row_copy(step, part, half, 0).wait_send()
+
+    def diagonal_copy(which, side):
+        lo, to = ((19, 1), (4, 22))[which]
+        return pltpu.make_async_remote_copy(
+            src_ref=rows_out.at[0, side, lo : lo + 3],
+            dst_ref=rows_in.at[0, side, to : to + 3],
+            send_sem=row_send.at[0, 1 + which, 0, side],
+            recv_sem=row_recv.at[0, 1 + which, 0, side],
+            device_id={"comp": partner, "band": band + 1 - 2 * side},
+            device_id_type=MESH,
+        )
 
     pieces = ((0, 2), (2, 3), (3, 4))
 
@@ -156,12 +167,13 @@
         def _(e):
             masked = state[0, e] * ocean[...]
             state[0, e] = masked
-            rows_out[0, 0, e] = masked[ROWS - 1 :, :]
-            rows_out[0, 1, e] = masked[:1, :]
-
-    load_spectrum.wait()
+            if lo == HALO:
+                rows_out[0, 0, e] = masked[ROWS - 1 :, :]
+                rows_out[0, 1, e] = masked[:1, :]
+
+    wait_bytes(state.at[0, HALO : HALO + OWN], spec_sem)
     mask_first(HALO, HALO + OWN)
-    pl.semaphore_wait(barrier, TILES - 1 + jnp.where(south, 1, 0) + jnp.where(north, 1, 0))
+    pl.semaphore_wait(barrier, TILES - 1 + jnp.where(south, 2, 0) + jnp.where(north, 2, 0))
 
     def cur_copy(t):
         return pltpu.make_async_remote_copy(
@@ -192,14 +204,20 @@
     pltpu.make_async_copy(cat, gathered.at[me], cur_recv).start()
 
     start_dirs(0)
+    for n in range(0, COMPS, LANES):
+        pltpu.make_async_copy(interp_any.at[n : n + LANES], interp.at[n : n + LANES], interp_sem).start()
 
     @pl.when(north)
     def _():
         beside_copy(0).start()
+        diagonal_copy(0, 0).start()
+        diagonal_copy(1, 0).start()
 
     @pl.when(south)
     def _():
         beside_copy(1).start()
+        diagonal_copy(0, 1).start()
+        diagonal_copy(1, 1).start()
 
     @pl.when(band == 0)
     def _():
@@ -226,14 +244,6 @@
         high = value.astype(bf16)
         split[part, rows, :] = high
         split[2 + part, rows, :] = (value - high.astype(f32)).astype(bf16)
-
-    load_interp.wait()
-
-    @pl.loop(0, COMPS // LANES)
-    def _(b):
-        span = pl.ds(pl.multiple_of(b * LANES, LANES), LANES)
-        store_split(0, span, interp[span, :])
-        store_split(1, span, interp[:, span].T)
 
     wait_bytes(gathered, cur_recv)
 
@@ -271,9 +281,9 @@
         ay = base_v[:, at] + speed * sine[direction]
         turn = turning[:, at] * cos_d
         change = (
-            jnp.maximum(ax, 0.0) * (centre - west) + jnp.minimum(ax, 0.0) * (east - centre)
-            + (jnp.maximum(ay, 0.0) * (centre - below) + jnp.minimum(ay, 0.0) * (above - centre))
-            + (jnp.maximum(turn, 0.0) * (centre - before) + jnp.minimum(turn, 0.0) * (after - centre))
+            ax * jnp.where(ax > 0.0, centre - west, east - centre)
+            + ay * jnp.where(ay > 0.0, centre - below, above - centre)
+            + turn * jnp.where(turn > 0.0, centre - before, after - centre)
         )
         return ocean[:, at] * (centre - change)
 
@@ -332,23 +342,36 @@
             finish_rows(step, inner, (half,))
             middle(step, 0, (half,))
             start_rows(step + 1, inner, (half,))
-        if step < 2:
-            start_dirs(step + 1)
+        if step:
+            start_dirs(step)
     for half in range(2):
         finish_rows(SUBSTEPS - 1, inner, (half,))
         last(0, (half,))
+    send_blocks(0, *INNER)
     for side in range(2):
         for n in range(3):
             dir_copy(side, n).wait()
     mask_first(0, HALO)
     mask_first(HALO + OWN, WIDE)
-    start_rows(0, sides)
-    send_blocks(0, *INNER)
+
+    @pl.when(south)
+    def _():
+        for which in range(2):
+            diagonal_copy(which, 0).wait_recv()
+            diagonal_copy(which, 1).wait_send()
+
+    @pl.when(north)
+    def _():
+        for which in range(2):
+            diagonal_copy(which, 1).wait_recv()
+            diagonal_copy(which, 0).wait_send()
+
     for step in range(SUBSTEPS - 1):
-        finish_rows(step, sides)
+        if step:
+            finish_rows(step, sides, (0, 1))
         middle(step, 1)
         middle(step, 2)
-        start_rows(step + 1, sides)
+        start_rows(step + 1, sides, (0, 1))
         send_blocks(step + 1, *INNER)
     finish_rows(SUBSTEPS - 1, sides)
     last(1)
@@ -356,6 +379,14 @@
     for group in range(4):
         send_blocks(group, 0, HALO)
         send_blocks(group, OWN - HALO, OWN)
+    wait_bytes(interp, interp_sem)
+
+    @pl.loop(0, COMPS // LANES)
+    def _(b):
+        span = pl.ds(pl.multiple_of(b * LANES, LANES), LANES)
+        store_split(0, span, interp[span, :])
+        store_split(1, span, interp[:, span].T)
+
     wait_bytes(recv1, in_recv)
 
     @pl.loop(0, COMPS // CHUNK)

time: 180 us -> 177 us (0.983)
  Pallas kernels: 174 us -> 171 us
    pallas_call x1, Pallas kernels: 174 us -> 171 us  [local(): pl.pallas_call(wave_kernel, out_shape=(jax.ShapeDtypeStruct((OWN, ROWS, L...]
where the time goes in v4:
time: 177 us
  Pallas kernels  171 us (97%)
  local copies, waits for them, and re-layouts  3.88 us (2%)
    pallas_call x1, Pallas kernels, local(): pl.pallas_call(wave_kernel, out_shape=(jax.ShapeDtypeStruct((OWN, ROWS, L...  171 us
    unnamed x4, local copies, waits for them, and re-layouts  3.88 us

profile of v4, /device:TPU:1, one launch (start us, length us, event | category | flops | bytes accessed | tf_op | source)
XLA Modules:
  0.0 177.2 jit_solution(742804526179722201)
XLA Ops:
  0.6 1.3 select_reduce_fusion.inverse
  1.9 171.4 %waves.1 = (f32[18,8,4096]{2,1,0:T(8,128)}, f32[2,8,64]{2,1,0:T(8,128)}) custom-call(f32[18,8,4096]{2,1,0:T(8,128)} %spectrum_any.1, f32[2,8,64]{2,1,0:T(8,128)} %currents.1, s32[32,4096]{1,0:T(8,128)} %sea.1, s32[32,4096]{1,0:T(8,128)} %classes.1, f32[1152,1152]{1,0:T(8,128)} %interp_any.1, f32[1152,2]{1,0:T(8,128)} %constant.10.clone.weights, ...), custom_call_target="tpu_custom_call" | custom-call | tf_op jit(solution)/shard_map/waves/pallas_call | solution.py:561
  173.4 0.0 copy-start
  173.4 3.3 %copy.16 = f32[18,8,4096]{2,1,0:T(8,128)} copy(f32[18,8,4096]{2,1,0:T(8,128)} %get-tuple-element.4) | data formatting | bytes 4718592
  176.6 0.0 copy-done
  176.6 0.6 copy.17
Async XLA Ops:
  173.4 3.3 %copy-start = (f32[2,8,64]{2,1,0:T(8,128)S(1)}, f32[2,8,64]{2,1,0:T(8,128)}, u32[]{:S(2)}) copy-start(f32[2,8,64]{2,1,0:T(8,128)} %get-tuple-element.5) | copy-start | bytes 12292

commit v5 on v4

--- a/solution.py
+++ b/solution.py
@@ -24,7 +24,7 @@
 CHUNK = 144
 POINTS = 512
 PIECE = 1024
-HALF = 2048
+HALF = 1024
 HALO = 4
 WIDE = OWN + 2 * HALO
 PAIRS = ((4, 0), (3, 7), (5, 1), (2, 6))
@@ -104,7 +104,7 @@
             device_id_type=MESH,
         )
 
-    def start_rows(step, parts, halves=(0, 1)):
+    def start_rows(step, parts, halves=(0, 1, 2, 3)):
         @pl.when(north)
         def _():
             for part in parts:
@@ -117,7 +117,7 @@
                 for half in halves:
                     row_copy(step, part, half, 1).start()
 
-    def finish_rows(step, parts, halves=(0, 1)):
+    def finish_rows(step, parts, halves=(0, 1, 2, 3)):
         @pl.when(south)
         def _():
             for part in parts:
@@ -287,24 +287,24 @@
         )
         return ocean[:, at] * (centre - change)
 
-    def middle(step, part, halves=(0, 1)):
+    def middle(step, part, halves=(0, 1, 2, 3)):
         lo, hi = span(step, part)
 
         @pl.loop(lo, hi)
         def _(e):
-            for piece in range(halves[0] * 2, halves[-1] * 2 + 2):
+            for piece in range(halves[0], halves[-1] + 1):
                 at = slice(piece * PIECE, (piece + 1) * PIECE)
                 new = advanced(step, e, piece)
                 state[step + 1, e, :, at] = new
                 rows_out[step + 1, 0, e, :, at] = new[ROWS - 1 :, :]
                 rows_out[step + 1, 1, e, :, at] = new[:1, :]
 
-    def last(part, halves=(0, 1)):
+    def last(part, halves=(0, 1, 2, 3)):
         lo, hi = span(SUBSTEPS - 1, part)
 
         @pl.loop(lo, hi)
         def _(e):
-            for piece in range(halves[0] * 2, halves[-1] * 2 + 2):
+            for piece in range(halves[0], halves[-1] + 1):
                 new = advanced(SUBSTEPS - 1, e, piece)
                 for tile in range(PIECE // LANES):
                     col = piece * (PIECE // LANES) + tile
@@ -338,13 +338,13 @@
 
     inner, sides = (0,), (1, 2)
     for step in range(SUBSTEPS - 1):
-        for half in range(2):
+        for half in range(4):
             finish_rows(step, inner, (half,))
             middle(step, 0, (half,))
             start_rows(step + 1, inner, (half,))
         if step:
             start_dirs(step)
-    for half in range(2):
+    for half in range(4):
         finish_rows(SUBSTEPS - 1, inner, (half,))
         last(0, (half,))
     send_blocks(0, *INNER)
@@ -368,10 +368,10 @@
 
     for step in range(SUBSTEPS - 1):
         if step:
-            finish_rows(step, sides, (0, 1))
+            finish_rows(step, sides, (0, 1, 2, 3))
         middle(step, 1)
         middle(step, 2)
-        start_rows(step + 1, sides, (0, 1))
+        start_rows(step + 1, sides, (0, 1, 2, 3))
         send_blocks(step + 1, *INNER)
     finish_rows(SUBSTEPS - 1, sides)
     last(1)
@@ -596,8 +596,8 @@
             dma,
             dma((2,)),
             dma((2,)),
-            dma((SUBSTEPS, 3, 2, 2)),
-            dma((SUBSTEPS, 3, 2, 2)),
+            dma((SUBSTEPS, 3, 4, 2)),
+            dma((SUBSTEPS, 3, 4, 2)),
             dma((2, 3)),
             dma((2, 3)),
             dma,

time: 177 us -> 177 us (level)
  no operation moved by 1% of the time
where the time goes in v5:
time: 177 us
  Pallas kernels  171 us (97%)
  local copies, waits for them, and re-layouts  3.88 us (2%)
    pallas_call x1, Pallas kernels, local(): pl.pallas_call(wave_kernel, out_shape=(jax.ShapeDtypeStruct((OWN, ROWS, L...  171 us
    unnamed x4, local copies, waits for them, and re-layouts  3.88 us

profile of v5, /device:TPU:1, one launch (start us, length us, event | category | flops | bytes accessed | tf_op | source)
XLA Modules:
  0.0 176.6 jit_solution(10611693191587308842)
XLA Ops:
  0.6 1.3 select_reduce_fusion.inverse
  1.9 170.8 %waves.1 = (f32[18,8,4096]{2,1,0:T(8,128)}, f32[2,8,64]{2,1,0:T(8,128)}) custom-call(f32[18,8,4096]{2,1,0:T(8,128)} %spectrum_any.1, f32[2,8,64]{2,1,0:T(8,128)} %currents.1, s32[32,4096]{1,0:T(8,128)} %sea.1, s32[32,4096]{1,0:T(8,128)} %classes.1, f32[1152,1152]{1,0:T(8,128)} %interp_any.1, f32[1152,2]{1,0:T(8,128)} %constant.10.clone.weights, ...), custom_call_target="tpu_custom_call" | custom-call | tf_op jit(solution)/shard_map/waves/pallas_call | solution.py:561
  172.7 0.0 copy-start
  172.8 3.3 %copy.16 = f32[18,8,4096]{2,1,0:T(8,128)} copy(f32[18,8,4096]{2,1,0:T(8,128)} %get-tuple-element.4) | data formatting | bytes 4718592
  176.0 0.0 copy-done
  176.0 0.6 copy.17
Async XLA Ops:
  172.7 3.3 %copy-start = (f32[2,8,64]{2,1,0:T(8,128)S(1)}, f32[2,8,64]{2,1,0:T(8,128)}, u32[]{:S(2)}) copy-start(f32[2,8,64]{2,1,0:T(8,128)} %get-tuple-element.5) | copy-start | bytes 12292

commit v6 on v5

--- a/solution.py
+++ b/solution.py
@@ -195,17 +195,15 @@
             device_id_type=MESH,
         )
 
-    start_rows(0, (0,))
 
     @pl.loop(1, TILES)
     def _(t):
         cur_copy(t).start()
 
     pltpu.make_async_copy(cat, gathered.at[me], cur_recv).start()
+    start_rows(0, (0,))
 
     start_dirs(0)
-    for n in range(0, COMPS, LANES):
-        pltpu.make_async_copy(interp_any.at[n : n + LANES], interp.at[n : n + LANES], interp_sem).start()
 
     @pl.when(north)
     def _():
@@ -348,6 +346,8 @@
         finish_rows(SUBSTEPS - 1, inner, (half,))
         last(0, (half,))
     send_blocks(0, *INNER)
+    for n in range(0, COMPS, LANES):
+        pltpu.make_async_copy(interp_any.at[n : n + LANES], interp.at[n : n + LANES], interp_sem).start()
     for side in range(2):
         for n in range(3):
             dir_copy(side, n).wait()

time: 177 us -> 177 us (level)
  no operation moved by 1% of the time
where the time goes in v6:
time: 177 us
  Pallas kernels  171 us (97%)
  local copies, waits for them, and re-layouts  3.88 us (2%)
    pallas_call x1, Pallas kernels, local(): pl.pallas_call(wave_kernel, out_shape=(jax.ShapeDtypeStruct((OWN, ROWS, L...  171 us
    unnamed x4, local copies, waits for them, and re-layouts  3.88 us

profile of v6, /device:TPU:1, one launch (start us, length us, event | category | flops | bytes accessed | tf_op | source)
XLA Modules:
  0.0 177.2 jit_solution(12163992785379220619)
XLA Ops:
  0.6 1.3 select_reduce_fusion.inverse
  1.9 171.4 %waves.1 = (f32[18,8,4096]{2,1,0:T(8,128)}, f32[2,8,64]{2,1,0:T(8,128)}) custom-call(f32[18,8,4096]{2,1,0:T(8,128)} %spectrum_any.1, f32[2,8,64]{2,1,0:T(8,128)} %currents.1, s32[32,4096]{1,0:T(8,128)} %sea.1, s32[32,4096]{1,0:T(8,128)} %classes.1, f32[1152,1152]{1,0:T(8,128)} %interp_any.1, f32[1152,2]{1,0:T(8,128)} %constant.10.clone.weights, ...), custom_call_target="tpu_custom_call" | custom-call | tf_op jit(solution)/shard_map/waves/pallas_call | solution.py:561
  173.3 0.0 copy-start
  173.3 3.3 %copy.16 = f32[18,8,4096]{2,1,0:T(8,128)} copy(f32[18,8,4096]{2,1,0:T(8,128)} %get-tuple-element.4) | data formatting | bytes 4718592
  176.6 0.0 copy-done
  176.6 0.6 copy.17
Async XLA Ops:
  173.3 3.3 %copy-start = (f32[2,8,64]{2,1,0:T(8,128)S(1)}, f32[2,8,64]{2,1,0:T(8,128)}, u32[]{:S(2)}) copy-start(f32[2,8,64]{2,1,0:T(8,128)} %get-tuple-element.5) | copy-start | bytes 12292
